TPU v7x, 32 devices: a whole 2x2x4 slice. The times are simulated.
32 devices in a mesh: seq: 8 (over z, y), tp: 4 (over x, core).
Axes of the slice: x: 2, y: 2, z: 4, core: 2. Of those that a mesh axis runs over, the one named last changes fastest.
Arguments:
- hidden_in: bfloat16 [1024, 1536], P('seq'), may hold values from -6 to 6
- w_query: bfloat16 [1536, 1536], P(None, 'tp'), may hold values from -0.625 to 0.625
- key_weight: bfloat16 [1536, 512], P(None, 'tp'), may hold values from -0.625 to 0.625
- value_weight: bfloat16 [1536, 512], P(None, 'tp'), may hold values from -0.15625 to 0.15625
- w_out: bfloat16 [1536, 1536], P('tp'), may hold values from -0.4375 to 0.4375
- cached_prefix_keys: bfloat16 [256, 512], P('seq', 'tp'), may hold values from -60000 to 60000
- cached_prefix_values: bfloat16 [256, 512], P('seq', 'tp'), may hold values from -6 to 6
- doc_ids: int32 [8, 128], P('seq'), may hold values from 0 to 3, never falling along the last dimension, each value on 1 to 64 neighbouring positions
- routes: int32 [1024, 8], P(('seq', 'tp')), may hold values from 0 to 31, all different within a row; in each aligned block of 32 rows (0 to 31, 32 to 63, ...) at most 16 rows name the same one
- gate_scores: float32 [1024, 8], P(('seq', 'tp')), may hold values from 0.2 to 1
- expert_in: bfloat16 [32, 1536, 1024], P('seq'), may hold values from -0.15625 to 0.15625
- expert_out: bfloat16 [32, 512, 1536], P('seq'), may hold values from -0.25 to 0.25
Outputs:
- attn_proj: bfloat16 [1024, 1536], P(('seq', 'tp'))
- expert_mix: bfloat16 [1024, 1536], P(('seq', 'tp'))
- layer_out: bfloat16 [1024, 1536], P(('seq', 'tp'))
Inputs may be any that keep to these rules, and one draw needn't show every extreme that they name: `routes`: within the rows of one device (aligned blocks of 32 tokens) no expert is picked by more than 16 tokens, a bound that some block reaches; every expert is picked somewhere.
All inputs are finite; a program needn't handle non-finite values.
Results may differ from a plain program's by a relative error of at most 0.028.
Values may be sent and summed in bfloat16 or wider, within the bound.
A program may use at most 64 MiB of HBM per device.

v0:
```python
import jax
import jax.numpy as jnp
from jax import lax
from jax.sharding import PartitionSpec as P

HEAD_WIDTH = 64
EXPERTS = 32


EPSILON = 1e-06
RESIDUAL = 0.22


def normalize(values):
    values = values.astype(jnp.float32)
    return values * lax.rsqrt(jnp.mean(values * values, axis=-1, keepdims=True) + EPSILON)


def rotary_apply(values, token_positions):
    half_size = values.shape[-1] // 2
    frequency = jnp.exp(
        -jnp.log(10000.0) * jnp.arange(half_size, dtype=jnp.float32) * 2.0 / values.shape[-1]
    )
    angles = token_positions[:, None] * frequency[None, :]
    cosine = jnp.cos(angles)[:, None, :]
    sine_part = jnp.sin(angles)[:, None, :]
    first_half = values[..., :half_size]
    second = values[..., half_size:]
    return jnp.concatenate(
        [first_half * cosine - second * sine_part, second * cosine + first_half * sine_part],
        axis=-1,
    )


def body(
    hidden_in,
    w_query,
    key_weight,
    value_weight,
    w_out,
    cached_prefix_keys,
    cached_prefix_values,
    doc_ids,
    routes,
    gate_scores,
    expert_in,
    expert_out,
):
    rows_dev = hidden_in.shape[0]
    column_list = hidden_in.shape[1]
    head_size = HEAD_WIDTH
    kv_local = key_weight.shape[1] // head_size
    group_width = w_query.shape[1] // head_size // kv_local
    seq_count = lax.axis_size("seq")
    prefix_len = cached_prefix_keys.shape[0] * seq_count
    doc_row = doc_ids[0]
    row_index = jnp.arange(rows_dev, dtype=jnp.int32)
    same_doc = doc_row[:, None] == doc_row[None, :]
    doc_start = jnp.min(jnp.where(same_doc, row_index[None, :], rows_dev), axis=1)
    token_positions = (prefix_len + row_index - doc_start).astype(jnp.float32)
    normed_input = normalize(hidden_in).astype(jnp.bfloat16)
    query_rows_all = jnp.dot(normed_input, w_query, preferred_element_type=jnp.float32).reshape(
        rows_dev, kv_local * group_width, head_size
    )
    query_rows_all = (
        rotary_apply(query_rows_all, token_positions)
        .astype(jnp.bfloat16)
        .reshape(rows_dev, kv_local, group_width, head_size)
    )
    fresh_key = jnp.dot(normed_input, key_weight, preferred_element_type=jnp.float32).reshape(
        rows_dev, kv_local, head_size
    )
    fresh_key = rotary_apply(fresh_key, token_positions).astype(jnp.bfloat16)
    fresh_value = (
        jnp.dot(normed_input, value_weight, preferred_element_type=jnp.float32)
        .astype(jnp.bfloat16)
        .reshape(rows_dev, kv_local, head_size)
    )
    own_scores = (
        jnp.einsum("tkgd,skd->tkgs", query_rows_all, fresh_key, preferred_element_type=jnp.float32)
        / head_size
    )
    visible = same_doc & (row_index[None, :] <= row_index[:, None])
    own_scores = jnp.where(visible[:, None, None, :], own_scores, -jnp.inf)
    row_top = jnp.max(own_scores, axis=-1)
    weights = jnp.exp(own_scores - row_top[..., None])
    denominator = jnp.sum(weights, axis=-1)
    numerator = jnp.einsum(
        "tkgs,skd->tkgd",
        weights.astype(jnp.bfloat16),
        fresh_value,
        preferred_element_type=jnp.float32,
    )
    running = (row_top, denominator, numerator)
    whole_keys, whole_values = (
        lax.all_gather(cached_prefix_keys, "seq", axis=0, tiled=True),
        lax.all_gather(cached_prefix_values, "seq", axis=0, tiled=True),
    )
    top_old, denom_old, numer_old = running
    key_rows = whole_keys.reshape(-1, kv_local, head_size)
    value_rows = whole_values.reshape(-1, kv_local, head_size)
    scores = (
        jnp.einsum("tkgd,pkd->tkgp", query_rows_all, key_rows, preferred_element_type=jnp.float32)
        / head_size
    )
    top_new = jnp.maximum(top_old, jnp.max(scores, axis=-1))
    shrink = jnp.exp(top_old - top_new)
    part_weights = jnp.exp(scores - top_new[..., None])
    denom_new = denom_old * shrink + jnp.sum(part_weights, axis=-1)
    numer_new = numer_old * shrink[..., None] + jnp.einsum(
        "tkgp,pkd->tkgd",
        part_weights.astype(jnp.bfloat16),
        value_rows,
        preferred_element_type=jnp.float32,
    )
    running = (top_new, denom_new, numer_new)
    attended = (
        (running[2] / running[1][..., None])
        .astype(jnp.bfloat16)
        .reshape(rows_dev, kv_local * group_width * head_size)
    )
    moe_rows = routes.shape[0]
    row_start = lax.axis_index("tp") * moe_rows
    summed_all = lax.psum(jnp.dot(attended, w_out, preferred_element_type=jnp.float32), "tp")
    attn_sum = lax.dynamic_slice_in_dim(summed_all, row_start, moe_rows, 0)
    residual = (
        lax.dynamic_slice_in_dim(hidden_in, row_start, moe_rows, 0).astype(jnp.float32)
        + RESIDUAL * attn_sum
    )
    routed = normalize(residual).astype(jnp.bfloat16)
    experts = EXPERTS
    units_dev = expert_in.shape[0]
    hparts = units_dev * seq_count // experts
    capacity = moe_rows // 2
    ff_part = expert_out.shape[1]
    onehot = (routes[:, :, None] == jnp.arange(experts, dtype=jnp.int32)[None, None, :]).astype(
        jnp.int32
    )
    per_row = jnp.sum(onehot, axis=1)
    before = jnp.cumsum(per_row, axis=0) - per_row
    rank_in = jnp.sum(onehot * before[:, None, :], axis=2)
    slot_of = routes * capacity + rank_in
    slot_ids = jnp.arange(experts * capacity, dtype=jnp.int32)
    pick_hit = slot_of[:, :, None] == slot_ids[None, None, :]
    selector = jnp.any(pick_hit, axis=1).T.astype(jnp.bfloat16)
    combiner = jnp.sum(jnp.where(pick_hit, gate_scores[:, :, None], 0.0), axis=1)
    gathered = jnp.dot(selector, routed, preferred_element_type=jnp.float32).astype(jnp.bfloat16)
    outgoing = jnp.broadcast_to(
        gathered.reshape(experts, 1, capacity, column_list),
        (experts, hparts, capacity, column_list),
    )
    outgoing = outgoing.reshape(seq_count, units_dev, capacity, column_list)
    gate_up = jnp.einsum(
        "sucd,udf->sucf",
        lax.all_to_all(outgoing, "seq", split_axis=0, concat_axis=0, tiled=True),
        expert_in,
        preferred_element_type=jnp.float32,
    )
    activated = (jax.nn.silu(gate_up[..., :ff_part]) * gate_up[..., ff_part:]).astype(jnp.bfloat16)
    partial_value = jnp.einsum(
        "sucf,ufd->sucd", activated, expert_out, preferred_element_type=jnp.float32
    ).astype(jnp.bfloat16)
    returned = lax.all_to_all(partial_value, "seq", split_axis=0, concat_axis=0, tiled=True)
    part_sum = jnp.sum(
        returned.reshape(experts, hparts, capacity, column_list).astype(jnp.float32), axis=1
    )
    part_sum = part_sum.reshape(experts * capacity, column_list)
    expert_sum = jnp.dot(
        combiner, part_sum, precision=lax.Precision.HIGHEST, preferred_element_type=jnp.float32
    )
    layer_out = (residual + RESIDUAL * expert_sum).astype(jnp.bfloat16)
    return (attn_sum.astype(jnp.bfloat16), expert_sum.astype(jnp.bfloat16), layer_out)


def solution(mesh):
    in_specs = (
        P("seq", None),
        P(None, "tp"),
        P(None, "tp"),
        P(None, "tp"),
        P("tp", None),
        P("seq", "tp"),
        P("seq", "tp"),
        P("seq", None),
        P(("seq", "tp"), None),
        P(("seq", "tp"), None),
        P("seq", None, None),
        P("seq", None, None),
    )
    out_specs = (P(("seq", "tp"), None), P(("seq", "tp"), None), P(("seq", "tp"), None))
    return jax.shard_map(body, mesh=mesh, in_specs=in_specs, out_specs=out_specs, check_vma=False)
```

profile of v0, /device:TPU:0, one launch (start us, length us, event | category | flops | bytes accessed | tf_op | source)
XLA Modules:
  0.0 217.8 jit_solution(4198426226496262772)
XLA Ops:
  7.2 0.0 copy-start
  7.2 0.0 copy-start.1
  7.2 0.0 copy-start.2
  7.2 0.0 all-reduce.2.cloned.1.call-start
  7.3 0.9 fusion.36
  8.2 0.8 compare_and_fusion
  9.0 1.2 fusion.22
  10.1 0.0 copy-start.5
  10.2 2.0 fusion.44
  12.2 0.0 copy-done.1
  12.2 0.0 copy-done.2
  12.2 0.0 copy-start.3
  12.2 0.3 fusion.46
  12.6 0.1 multiply_cosine_fusion
  12.7 0.0 copy-start.6
  12.8 0.0 copy-done.5
  12.8 32.3 %all_gather.6 = bf16[256,128]{1,0:T(8,128)(2,1)S(1)} all-gather(bf16[32,128]{1,0:T(8,128)(2,1)S(1)} %copy-done.5), channel_id=1, replica_groups=mesh['seq'=8,'tp'=4] {'seq'}, dimensions={0}, use_global_device_ids=true | all-gather | bytes 73728 | tf_op jit(solution)/shard_map/all_gather | solution.py:96
  45.1 0.1 copy.55
  45.2 0.4 fusion.50
  45.6 0.3 fusion.49
  45.9 0.1 fusion.31
  46.0 0.0 copy-done.3
  46.0 0.4 convolution_convert_fusion.1
  46.4 0.0 copy-done.6
  46.4 30.5 %all_gather.7 = bf16[256,128]{1,0:T(8,128)(2,1)S(1)} all-gather(bf16[32,128]{1,0:T(8,128)(2,1)S(1)} %copy-done.6), channel_id=1, replica_groups=mesh['seq'=8,'tp'=4] {'seq'}, dimensions={0}, use_global_device_ids=true | all-gather | bytes 73728 | tf_op jit(solution)/shard_map/all_gather | solution.py:97
  76.9 0.1 copy.56
  77.0 0.3 fusion.24
  77.3 0.2 fusion.19
  77.5 0.3 fusion.20
  77.9 0.0 copy-start.4
  77.9 0.0 copy-done
  77.9 1.3 fusion.51
  79.2 0.0 all-reduce.2.cloned.1.call-update
  79.2 0.0 copy-done.4
  79.2 0.1 copy.57
  79.3 0.1 convert_reduce_fusion
  79.4 0.1 reduce_window_sum.11
  79.4 0.7 select_reduce_fusion.1
  80.1 0.1 copy.58
  80.2 0.1 copy.59
  80.3 0.2 fusion.28
  80.5 34.3 %all-reduce.2.cloned.1.call-done = f32[128,1536]{1,0:T(8,128)} async-done(((f32[128,1536]{1,0:T(8,128)}), f32[128,1536]{1,0:T(8,128)}) %all-reduce.2.cloned.1.call-update) | async-done | bytes 786448 | tf_op jit(solution)/shard_map/psum | solution.py:124
  114.9 1.1 multiply_reduce_fusion
  115.9 1.6 convolution_convert_fusion
  117.5 0.0 slice-start
  117.5 41.8 %all_to_all.10 = bf16[8,4,16,1536]{3,2,1,0:T(8,128)(2,1)S(1)} all-to-all(bf16[8,4,16,1536]{3,2,1,0:T(8,128)(2,1)S(1)} %bitcast.80), channel_id=1, replica_groups=mesh['seq'=8,'tp'=4] {'seq'}, dimensions={0} | all-to-all | bytes 3145728 | tf_op jit(solution)/shard_map/all_to_all | solution.py:155
  159.3 0.0 slice-start.1
  159.3 6.5 %fusion.10 = f32[8,4,16,1024]{3,2,0,1:T(8,128)S(1)} fusion(bf16[4,1536,1024]{2,1,0:T(8,128)(2,1)} %param.22, bf16[8,4,16,1536]{3,2,1,0:T(8,128)(2,1)S(1)} %all_to_all.10), kind=kOutput, calls=%fused_computation.7 | convolution fusion | flops 1610612736 | bytes 16252928 | tf_op jit(solution)/shard_map/sucd,udf->sucf/dot_general | solution.py:153
  165.8 0.0 slice-done
  165.8 0.0 slice-done.1
  165.9 1.1 fusion.7
  167.0 1.3 copy.62
  168.3 0.0 copy-start.7
  168.3 3.7 %all-to-all-start.1 = ((bf16[8,4,16,1536]{3,2,1,0:T(8,128)(2,1)}), bf16[8,4,16,1536]{3,2,1,0:T(8,128)(2,1)S(1)}, u32[]{:S(2)}, u32[]{:S(2)}) async-start(bf16[8,4,16,1536]{3,2,1,0:T(8,128)(2,1)} %copy.62), calls=%async_computation.1 | async-start | bytes 3145728 | tf_op jit(solution)/shard_map/all_to_all | solution.py:163
  172.0 0.0 copy-done.7
  172.0 0.1 copy.60
  172.1 0.2 select_reduce_fusion
  172.3 1.6 dynamic-slice_convert_fusion
  173.9 34.6 %all-to-all-done.1 = bf16[8,4,16,1536]{3,2,1,0:T(8,128)(2,1)S(1)} async-done(((bf16[8,4,16,1536]{3,2,1,0:T(8,128)(2,1)}), bf16[8,4,16,1536]{3,2,1,0:T(8,128)(2,1)S(1)}, u32[]{:S(2)}, u32[]{:S(2)}) %all-to-all-start.1) | async-done | bytes 1572896 | tf_op jit(solution)/shard_map/all_to_all | solution.py:163
  208.5 2.5 %add_convert_fusion = (bf16[32,1536]{1,0:T(8,128)(2,1)}, bf16[32,1536]{1,0:T(8,128)(2,1)}) fusion(f32[128,1536]{1,0:T(8,128)} %all-reduce.2.cloned.1.call-done, s32[]{:T(128)S(6)} %select_n.18, bf16[128,1536]{1,0:T(8,128)(2,1)S(1)} %copy-done.1, f32[32,512]{1,0:T(8,128)S(1)} %select_reduce_fusion, bf16[512,1536]{1,0:T(8,128)(2,1)S(1)} %bitcast.79), kind=kOutput, calls=%fused_computation.38 | convolution fusion | flops 302333952 | bytes 2129924 | tf_op jit(solution)/shard_map/dot_general | solution.py:168
  (11 shorter events, 0.1 us)
Async XLA Ops:
  7.2 70.7 %copy-start = (bf16[384,1536]{1,0:T(8,128)(2,1)S(1)}, bf16[384,1536]{1,0:T(8,128)(2,1)}, u32[]{:S(2)}) copy-start(bf16[384,1536]{1,0:T(8,128)(2,1)} %param.16) | copy-start | bytes 3538948
  7.2 5.0 %copy-start.1 = (bf16[128,1536]{1,0:T(8,128)(2,1)S(1)}, bf16[128,1536]{1,0:T(8,128)(2,1)}, u32[]{:S(2)}) copy-start(bf16[128,1536]{1,0:T(8,128)(2,1)} %param.12) | copy-start | bytes 1179652
  7.2 5.0 %copy-start.2 = (bf16[1536,128]{1,0:T(8,128)(2,1)S(1)}, bf16[1536,128]{1,0:T(8,128)(2,1)}, u32[]{:S(2)}) copy-start(bf16[1536,128]{1,0:T(8,128)(2,1)} %param.14) | copy-start | bytes 1179652
  7.2 107.7 %all-reduce.2.cloned.1.call-start = ((), (), s32[]{:S(2)}) async-start(), calls=%async_computation.2 | async-start | bytes 1572864 | tf_op jit(solution)/shard_map/psum | solution.py:124
  10.1 2.6 %copy-start.5 = (bf16[32,128]{1,0:T(8,128)(2,1)S(1)}, bf16[32,128]{1,0:T(8,128)(2,1)}, u32[]{:S(2)}) copy-start(bf16[32,128]{1,0:T(8,128)(2,1)} %param.17) | copy-start | bytes 24580
  12.2 33.8 %copy-start.3 = (bf16[1536,128]{1,0:T(8,128)(2,1)S(1)}, bf16[1536,128]{1,0:T(8,128)(2,1)}, u32[]{:S(2)}) copy-start(bf16[1536,128]{1,0:T(8,128)(2,1)} %param.15) | copy-start | bytes 1179652
  12.7 33.6 %copy-start.6 = (bf16[32,128]{1,0:T(8,128)(2,1)S(1)}, bf16[32,128]{1,0:T(8,128)(2,1)}, u32[]{:S(2)}) copy-start(bf16[32,128]{1,0:T(8,128)(2,1)} %param.18) | copy-start | bytes 24580
  77.9 1.3 copy-start.4
  117.5 48.3 %slice-start = ((s8[6291456]{0:T(1024)(128)(4,1)}), s8[4194304]{0:T(1024)(128)(4,1)S(1)}, s32[]{:S(2)}) async-start(s8[6291456]{0:T(1024)(128)(4,1)} %bitcast.93), calls=%async_computation.3 | async-start | bytes 8388608
  159.3 6.5 %slice-start.1 = ((s8[6291456]{0:T(1024)(128)(4,1)}), s8[2097152]{0:T(1024)(128)(4,1)S(1)}, s32[]{:S(2)}) async-start(s8[6291456]{0:T(1024)(128)(4,1)} %bitcast.93), calls=%async_computation.4 | async-start | bytes 4194304
  168.3 3.7 %copy-start.7 = (f32[32,8]{0,1:T(8,128)S(1)}, f32[32,8]{0,1:T(8,128)}, u32[]{:S(2)}) copy-start(f32[32,8]{0,1:T(8,128)} %param.21) | copy-start | bytes 3076
  168.3 40.2 %all-to-all-start.1 = ((bf16[8,4,16,1536]{3,2,1,0:T(8,128)(2,1)}), bf16[8,4,16,1536]{3,2,1,0:T(8,128)(2,1)S(1)}, u32[]{:S(2)}, u32[]{:S(2)}) async-start(bf16[8,4,16,1536]{3,2,1,0:T(8,128)(2,1)} %copy.62), calls=%async_computation.1 | async-start | bytes 3145728 | tf_op jit(solution)/shard_map/all_to_all | solution.py:163
Sparse Core Ops, SparseCore 0:
  79.3 35.5 all-reduce.1
where the time goes:
time: 218 us
  blocking collectives  105 us (48%)
  waiting for transfers between devices  68.9 us (32%)
  matrix products  16.9 us (8%)
  between operations  14.4 us (7%)
  other arithmetic  5.89 us (3%)
  starting transfers between devices  3.75 us (2%)
  local copies, waits for them, and re-layouts  3.43 us (2%)
    all_to_all x1, blocking collectives, body(): lax.all_to_all(outgoing, 'seq', split_axis=0, concat_axis=0, tiled=True)  41.8 us
    all_to_all x1, waiting for transfers between devices, body(): lax.all_to_all(partial_value, 'seq', split_axis=0, concat_axis=0, tiled=T...  34.6 us
    psum x1, waiting for transfers between devices, body(): lax.psum(jnp.dot(attended, w_out, preferred_element_type=jnp.float32), 'tp')  34.3 us
    all_gather x1, blocking collectives, body(): lax.all_gather(cached_prefix_keys, 'seq', axis=0, tiled=True)  32.3 us
    all_gather x1, blocking collectives, body(): lax.all_gather(cached_prefix_values, 'seq', axis=0, tiled=True)  30.5 us
    dot_general x1, matrix products, body(): jnp.einsum('sucd,udf->sucf', lax.all_to_all(outgoing, 'seq', split_axis=0...  6.52 us
  transfers between devices with their start and end apart: 2, of which 2 were waited for; matrix products, arithmetic and copies ran while one was open for 1% of the time, Pallas kernels for 0%

commit v1 on v0

--- a/solution.py
+++ b/solution.py
@@ -137,7 +137,10 @@
         jnp.int32
     )
     per_row = jnp.sum(onehot, axis=1)
-    before = jnp.cumsum(per_row, axis=0) - per_row
+    earlier = (jnp.arange(moe_rows)[None, :] < jnp.arange(moe_rows)[:, None]).astype(jnp.bfloat16)
+    before = jnp.dot(
+        earlier, per_row.astype(jnp.bfloat16), preferred_element_type=jnp.float32
+    ).astype(jnp.int32)
     rank_in = jnp.sum(onehot * before[:, None, :], axis=2)
     slot_of = routes * capacity + rank_in
     slot_ids = jnp.arange(experts * capacity, dtype=jnp.int32)

time: 218 us -> 218 us (level)
  no operation moved by 1% of the time
where the time goes in v1:
time: 218 us
  blocking collectives  105 us (48%)
  waiting for transfers between devices  68.9 us (32%)
  matrix products  17 us (8%)
  between operations  14.4 us (7%)
  other arithmetic  5.82 us (3%)
  starting transfers between devices  3.75 us (2%)
  local copies, waits for them, and re-layouts  3.43 us (2%)
    all_to_all x1, blocking collectives, body(): lax.all_to_all(outgoing, 'seq', split_axis=0, concat_axis=0, tiled=True)  41.8 us
    all_to_all x1, waiting for transfers between devices, body(): lax.all_to_all(partial_value, 'seq', split_axis=0, concat_axis=0, tiled=T...  34.6 us
    psum x1, waiting for transfers between devices, body(): lax.psum(jnp.dot(attended, w_out, preferred_element_type=jnp.float32), 'tp')  34.3 us
    all_gather x1, blocking collectives, body(): lax.all_gather(cached_prefix_keys, 'seq', axis=0, tiled=True)  32.3 us
    all_gather x1, blocking collectives, body(): lax.all_gather(cached_prefix_values, 'seq', axis=0, tiled=True)  30.5 us
    dot_general x1, matrix products, body(): jnp.einsum('sucd,udf->sucf', lax.all_to_all(outgoing, 'seq', split_axis=0...  6.52 us
  transfers between devices with their start and end apart: 2, of which 2 were waited for; matrix products, arithmetic and copies ran while one was open for 1% of the time, Pallas kernels for 0%

profile of v1, /device:TPU:0, one launch (start us, length us, event | category | flops | bytes accessed | tf_op | source)
XLA Modules:
  0.0 217.8 jit_solution(12185322112428728234)
XLA Ops:
  7.2 0.0 copy-start
  7.2 0.0 copy-start.1
  7.2 0.0 copy-start.2
  7.2 0.0 all-reduce.2.cloned.1.call-start
  7.3 0.9 fusion.36
  8.2 0.8 compare_and_fusion
  9.0 1.2 fusion.22
  10.1 0.0 copy-start.5
  10.2 2.0 fusion.45
  12.2 0.0 copy-done.1
  12.2 0.0 copy-done.2
  12.2 0.0 copy-start.3
  12.2 0.3 fusion.47
  12.6 0.1 multiply_cosine_fusion
  12.7 0.0 copy-start.6
  12.8 0.0 copy-done.5
  12.8 32.3 %all_gather.6 = bf16[256,128]{1,0:T(8,128)(2,1)S(1)} all-gather(bf16[32,128]{1,0:T(8,128)(2,1)S(1)} %copy-done.5), channel_id=1, replica_groups=mesh['seq'=8,'tp'=4] {'seq'}, dimensions={0}, use_global_device_ids=true | all-gather | bytes 73728 | tf_op jit(solution)/shard_map/all_gather | solution.py:96
  45.1 0.1 copy.55
  45.2 0.4 fusion.51
  45.6 0.3 fusion.50
  45.9 0.1 fusion.31
  46.0 0.0 copy-done.3
  46.0 0.4 convolution_convert_fusion.1
  46.4 0.0 copy-done.6
  46.4 30.5 %all_gather.7 = bf16[256,128]{1,0:T(8,128)(2,1)S(1)} all-gather(bf16[32,128]{1,0:T(8,128)(2,1)S(1)} %copy-done.6), channel_id=1, replica_groups=mesh['seq'=8,'tp'=4] {'seq'}, dimensions={0}, use_global_device_ids=true | all-gather | bytes 73728 | tf_op jit(solution)/shard_map/all_gather | solution.py:97
  76.9 0.1 copy.56
  77.0 0.3 fusion.24
  77.3 0.2 fusion.19
  77.5 0.3 fusion.20
  77.9 0.0 copy-start.4
  77.9 0.0 copy-done
  77.9 1.3 fusion.52
  79.2 0.0 all-reduce.2.cloned.1.call-update
  79.2 0.0 copy-done.4
  79.2 0.1 copy.57
  79.3 0.1 convert_reduce_fusion
  79.4 0.1 convolution_convert_fusion.2
  79.5 0.7 select_reduce_fusion.1
  80.2 0.1 copy.58
  80.3 0.1 copy.59
  80.3 0.2 fusion.28
  80.6 34.3 %all-reduce.2.cloned.1.call-done = f32[128,1536]{1,0:T(8,128)} async-done(((f32[128,1536]{1,0:T(8,128)}), f32[128,1536]{1,0:T(8,128)}) %all-reduce.2.cloned.1.call-update) | async-done | bytes 786448 | tf_op jit(solution)/shard_map/psum | solution.py:124
  114.9 1.1 multiply_reduce_fusion
  116.0 1.6 convolution_convert_fusion
  117.6 0.0 slice-start
  117.6 41.8 %all_to_all.10 = bf16[8,4,16,1536]{3,2,1,0:T(8,128)(2,1)S(1)} all-to-all(bf16[8,4,16,1536]{3,2,1,0:T(8,128)(2,1)S(1)} %bitcast.80), channel_id=1, replica_groups=mesh['seq'=8,'tp'=4] {'seq'}, dimensions={0} | all-to-all | bytes 3145728 | tf_op jit(solution)/shard_map/all_to_all | solution.py:158
  159.4 0.0 slice-start.1
  159.4 6.5 %fusion.10 = f32[8,4,16,1024]{3,2,0,1:T(8,128)S(1)} fusion(bf16[4,1536,1024]{2,1,0:T(8,128)(2,1)} %param.22, bf16[8,4,16,1536]{3,2,1,0:T(8,128)(2,1)S(1)} %all_to_all.10), kind=kOutput, calls=%fused_computation.7 | convolution fusion | flops 1610612736 | bytes 16252928 | tf_op jit(solution)/shard_map/sucd,udf->sucf/dot_general | solution.py:156
  165.9 0.0 slice-done
  165.9 0.0 slice-done.1
  165.9 1.1 fusion.7
  167.1 1.3 copy.62
  168.3 0.0 copy-start.7
  168.3 3.7 %all-to-all-start.1 = ((bf16[8,4,16,1536]{3,2,1,0:T(8,128)(2,1)}), bf16[8,4,16,1536]{3,2,1,0:T(8,128)(2,1)S(1)}, u32[]{:S(2)}, u32[]{:S(2)}) async-start(bf16[8,4,16,1536]{3,2,1,0:T(8,128)(2,1)} %copy.62), calls=%async_computation.1 | async-start | bytes 3145728 | tf_op jit(solution)/shard_map/all_to_all | solution.py:166
  172.1 0.0 copy-done.7
  172.1 0.1 copy.60
  172.1 0.2 select_reduce_fusion
  172.4 1.6 dynamic-slice_convert_fusion
  174.0 34.6 %all-to-all-done.1 = bf16[8,4,16,1536]{3,2,1,0:T(8,128)(2,1)S(1)} async-done(((bf16[8,4,16,1536]{3,2,1,0:T(8,128)(2,1)}), bf16[8,4,16,1536]{3,2,1,0:T(8,128)(2,1)S(1)}, u32[]{:S(2)}, u32[]{:S(2)}) %all-to-all-start.1) | async-done | bytes 1572896 | tf_op jit(solution)/shard_map/all_to_all | solution.py:166
  208.5 2.5 %add_convert_fusion = (bf16[32,1536]{1,0:T(8,128)(2,1)}, bf16[32,1536]{1,0:T(8,128)(2,1)}) fusion(f32[128,1536]{1,0:T(8,128)} %all-reduce.2.cloned.1.call-done, s32[]{:T(128)S(6)} %select_n.18, bf16[128,1536]{1,0:T(8,128)(2,1)S(1)} %copy-done.1, f32[32,512]{1,0:T(8,128)S(1)} %select_reduce_fusion, bf16[512,1536]{1,0:T(8,128)(2,1)S(1)} %bitcast.79), kind=kOutput, calls=%fused_computation.39 | convolution fusion | flops 302333952 | bytes 2129924 | tf_op jit(solution)/shard_map/dot_general | solution.py:171
  (10 shorter events, 0.1 us)
Async XLA Ops:
  7.2 70.7 %copy-start = (bf16[384,1536]{1,0:T(8,128)(2,1)S(1)}, bf16[384,1536]{1,0:T(8,128)(2,1)}, u32[]{:S(2)}) copy-start(bf16[384,1536]{1,0:T(8,128)(2,1)} %param.16) | copy-start | bytes 3538948
  7.2 5.0 %copy-start.1 = (bf16[128,1536]{1,0:T(8,128)(2,1)S(1)}, bf16[128,1536]{1,0:T(8,128)(2,1)}, u32[]{:S(2)}) copy-start(bf16[128,1536]{1,0:T(8,128)(2,1)} %param.12) | copy-start | bytes 1179652
  7.2 5.0 %copy-start.2 = (bf16[1536,128]{1,0:T(8,128)(2,1)S(1)}, bf16[1536,128]{1,0:T(8,128)(2,1)}, u32[]{:S(2)}) copy-start(bf16[1536,128]{1,0:T(8,128)(2,1)} %param.14) | copy-start | bytes 1179652
  7.2 107.7 %all-reduce.2.cloned.1.call-start = ((), (), s32[]{:S(2)}) async-start(), calls=%async_computation.2 | async-start | bytes 1572864 | tf_op jit(solution)/shard_map/psum | solution.py:124
  10.1 2.6 %copy-start.5 = (bf16[32,128]{1,0:T(8,128)(2,1)S(1)}, bf16[32,128]{1,0:T(8,128)(2,1)}, u32[]{:S(2)}) copy-start(bf16[32,128]{1,0:T(8,128)(2,1)} %param.17) | copy-start | bytes 24580
  12.2 33.8 %copy-start.3 = (bf16[1536,128]{1,0:T(8,128)(2,1)S(1)}, bf16[1536,128]{1,0:T(8,128)(2,1)}, u32[]{:S(2)}) copy-start(bf16[1536,128]{1,0:T(8,128)(2,1)} %param.15) | copy-start | bytes 1179652
  12.7 33.6 %copy-start.6 = (bf16[32,128]{1,0:T(8,128)(2,1)S(1)}, bf16[32,128]{1,0:T(8,128)(2,1)}, u32[]{:S(2)}) copy-start(bf16[32,128]{1,0:T(8,128)(2,1)} %param.18) | copy-start | bytes 24580
  77.9 1.3 copy-start.4
  117.6 48.3 %slice-start = ((s8[6291456]{0:T(1024)(128)(4,1)}), s8[4194304]{0:T(1024)(128)(4,1)S(1)}, s32[]{:S(2)}) async-start(s8[6291456]{0:T(1024)(128)(4,1)} %bitcast.93), calls=%async_computation.3 | async-start | bytes 8388608
  159.4 6.5 %slice-start.1 = ((s8[6291456]{0:T(1024)(128)(4,1)}), s8[2097152]{0:T(1024)(128)(4,1)S(1)}, s32[]{:S(2)}) async-start(s8[6291456]{0:T(1024)(128)(4,1)} %bitcast.93), calls=%async_computation.4 | async-start | bytes 4194304
  168.3 3.7 %copy-start.7 = (f32[32,8]{0,1:T(8,128)S(1)}, f32[32,8]{0,1:T(8,128)}, u32[]{:S(2)}) copy-start(f32[32,8]{0,1:T(8,128)} %param.21) | copy-start | bytes 3076
  168.3 40.2 %all-to-all-start.1 = ((bf16[8,4,16,1536]{3,2,1,0:T(8,128)(2,1)}), bf16[8,4,16,1536]{3,2,1,0:T(8,128)(2,1)S(1)}, u32[]{:S(2)}, u32[]{:S(2)}) async-start(bf16[8,4,16,1536]{3,2,1,0:T(8,128)(2,1)} %copy.62), calls=%async_computation.1 | async-start | bytes 3145728 | tf_op jit(solution)/shard_map/all_to_all | solution.py:166
Sparse Core Ops, SparseCore 0:
  79.3 35.5 all-reduce.1

commit v2 on v0

v2 whole, which is shorter than its diff:
```python
import functools

import jax
import jax.numpy as jnp
from jax import lax
from jax.experimental import pallas as pl
from jax.experimental.pallas import tpu as pltpu
from jax.sharding import PartitionSpec as P

HEAD_WIDTH = 64
EXPERTS = 32
EPSILON = 1e-06
RESIDUAL = 0.22
MESH = pl.DeviceIdType.MESH
F32 = jnp.float32
BF16 = jnp.bfloat16


def normalize(values):
    values = values.astype(F32)
    return values * lax.rsqrt(jnp.mean(values * values, axis=-1, keepdims=True) + EPSILON)


def rotary_apply(values, token_positions):
    half_size = values.shape[-1] // 2
    frequency = jnp.exp(
        -jnp.log(10000.0) * jnp.arange(half_size, dtype=F32) * 2.0 / values.shape[-1]
    )
    angles = token_positions[:, None] * frequency[None, :]
    cosine = jnp.cos(angles)[:, None, :]
    sine_part = jnp.sin(angles)[:, None, :]
    first_half = values[..., :half_size]
    second = values[..., half_size:]
    return jnp.concatenate(
        [first_half * cosine - second * sine_part, second * cosine + first_half * sine_part],
        axis=-1,
    )


def each(start, stop, fn):
    if stop - start <= 8:
        for i in range(start, stop):
            fn(i)
    else:

        @pl.loop(start, stop)
        def _(i):
            fn(i)


def peers(n):
    half = n // 2
    me = lax.axis_index("seq")
    high, low = me // 2, lax.rem(me, 2)

    def ahead(side, step):
        place = low if side == 0 else 1 - low
        return {"seq": lax.rem(high + step, half) * 2 + place}

    def behind(side, step):
        place = low if side == 0 else 1 - low
        return {"seq": lax.rem(high + half - step, half) * 2 + place}

    return half, ahead, behind


def gather_kernel(n, kv_ref, gate_ref, kv_all, gate_all, send, recv, local):
    half, ahead, _ = peers(n)
    own_a = pltpu.make_async_copy(kv_ref, kv_all.at[0, 0], local.at[0])
    own_b = pltpu.make_async_copy(gate_ref, gate_all.at[0, 0], local.at[1])
    own_a.start()
    own_b.start()
    barrier = pltpu.get_barrier_semaphore()

    def greet(side, step):
        pl.semaphore_signal(barrier, inc=1, device_id=ahead(side, step), device_id_type=MESH)

    each(1, half, lambda step: greet(0, step))
    each(0, half, lambda step: greet(1, step))
    pl.semaphore_wait(barrier, n - 1)

    def copies(side, step):
        return [
            pltpu.make_async_remote_copy(
                src_ref=src,
                dst_ref=dst.at[side, step],
                send_sem=send.at[kind, side, step],
                recv_sem=recv.at[kind, side, step],
                device_id=ahead(side, step),
                device_id_type=MESH,
            )
            for kind, (src, dst) in enumerate(((kv_ref, kv_all), (gate_ref, gate_all)))
        ]

    def start(side, step):
        for c in copies(side, step):
            c.start()

    def finish(side, step):
        for c in copies(side, step):
            c.wait()

    each(1, half, lambda step: start(0, step))
    each(0, half, lambda step: start(1, step))
    each(1, half, lambda step: finish(0, step))
    each(0, half, lambda step: finish(1, step))
    own_a.wait()
    own_b.wait()


def gather(n, kv, gates):
    half = n // 2
    vmem = pl.BlockSpec(memory_space=pltpu.VMEM)
    return pl.pallas_call(
        functools.partial(gather_kernel, n),
        out_shape=(
            jax.ShapeDtypeStruct((2, half) + kv.shape, kv.dtype),
            jax.ShapeDtypeStruct((2, half) + gates.shape, gates.dtype),
        ),
        in_specs=[vmem, vmem],
        out_specs=(vmem, vmem),
        scratch_shapes=[
            pltpu.SemaphoreType.DMA((2, 2, half)),
            pltpu.SemaphoreType.DMA((2, 2, half)),
            pltpu.SemaphoreType.DMA((2,)),
        ],
        compiler_params=pltpu.CompilerParams(
            collective_id=0, has_side_effects=True, vmem_limit_bytes=32 << 20
        ),
    )(kv, gates)


def tail_kernel(
    n, n_tp, hparts,
    attended, w_out, hidden, gate_all, in_hbm, out_hbm,
    proj_ref, mix_ref, layer_ref,
    w_in, w_back, sums, outbox, inbox, tok, part, acc, cross, cross_in, home, home_in,
    w_sem, tp_send, tp_recv, tok_send, tok_recv, x_send, x_recv, h_send, h_recv,
):
    half, ahead, behind = peers(n)
    units, ff = out_hbm.shape[0], out_hbm.shape[1]
    rows, width = proj_ref.shape
    me_tp = lax.axis_index("tp")
    chunk = min(4, half)

    def fetch(u):
        return (
            pltpu.make_async_copy(in_hbm.at[u], w_in.at[u], w_sem.at[0, u]),
            pltpu.make_async_copy(out_hbm.at[u], w_back.at[u], w_sem.at[1, u]),
        )

    barrier = pltpu.get_barrier_semaphore()

    def greet(where):
        pl.semaphore_signal(barrier, inc=1, device_id=where, device_id_type=MESH)

    def tp_peer(t):
        return lax.rem(me_tp + t, n_tp)

    each(1, n_tp, lambda t: greet({"tp": tp_peer(t)}))
    each(1, half, lambda d: greet(ahead(0, d)))
    greet(ahead(1, 0))
    for u in range(units):
        for c in fetch(u):
            c.start()
    whole = jnp.dot(attended[...], w_out[...], preferred_element_type=F32)
    sums[...] = whole
    outbox[...] = whole.astype(BF16)
    pl.semaphore_wait(barrier, n_tp - 1 + half)

    def tp_copy(t):
        return pltpu.make_async_remote_copy(
            src_ref=outbox.at[pl.ds(pl.multiple_of(tp_peer(t) * rows, rows), rows)],
            dst_ref=inbox.at[t],
            send_sem=tp_send.at[t],
            recv_sem=tp_recv.at[t],
            device_id={"tp": tp_peer(t)},
            device_id_type=MESH,
        )

    each(1, n_tp, lambda t: tp_copy(t).start())
    mine = pl.ds(pl.multiple_of(me_tp * rows, rows), rows)
    attn_sum = sums[mine, :]
    for t in range(1, n_tp):
        tp_copy(t).wait_recv()
        attn_sum = attn_sum + inbox[t].astype(F32)
    residual = hidden[mine, :].astype(F32) + RESIDUAL * attn_sum
    proj_ref[...] = attn_sum.astype(BF16)
    tok[0, 0] = normalize(residual).astype(BF16)

    def tok_copy(d):
        return pltpu.make_async_remote_copy(
            src_ref=tok.at[0, 0],
            dst_ref=tok.at[0, d],
            send_sem=tok_send.at[0, d],
            recv_sem=tok_recv.at[0, d],
            device_id=ahead(0, d),
            device_id_type=MESH,
        )

    def tok_cross(d):
        return pltpu.make_async_remote_copy(
            src_ref=tok.at[0, d],
            dst_ref=tok.at[1, d],
            send_sem=tok_send.at[1, d],
            recv_sem=tok_recv.at[1, d],
            device_id=ahead(1, 0),
            device_id_type=MESH,
        )

    def relay(d):
        tok_copy(d).wait_recv()
        tok_cross(d).start()

    each(1, half, lambda d: tok_copy(d).start())
    tok_cross(0).start()
    for u in range(units):
        for c in fetch(u):
            c.wait()
    each(1, half, relay)

    first_unit = lax.axis_index("seq") * units

    def experts(side, begin):
        tokens = tok[side, pl.ds(begin, chunk)].reshape(chunk * rows, width)
        gates = gate_all[side, pl.ds(begin, chunk)].reshape(chunk * rows, gate_all.shape[-1])
        lanes = lax.broadcasted_iota(jnp.int32, gates.shape, 1)
        acc[...] = jnp.zeros(acc.shape, F32)

        @pl.loop(0, units)
        def _(u):
            expert = (first_unit + u) // hparts
            weight = jnp.sum(jnp.where(lanes == expert, gates, 0.0), axis=1, keepdims=True)
            gate_up = jnp.dot(tokens, w_in[u], preferred_element_type=F32)
            active = (jax.nn.silu(gate_up[:, :ff]) * gate_up[:, ff:]).astype(BF16)
            back = jnp.dot(active, w_back[u], preferred_element_type=F32).astype(BF16)
            acc[...] += weight * back.astype(F32)

        total = acc[...].reshape(chunk, rows, width)
        if side == 0:
            part[pl.ds(begin, chunk)] = total
        else:
            cross[pl.ds(begin, chunk)] = total.astype(BF16)

    each(0, half // chunk, lambda c: experts(0, c * chunk))

    def cross_copy(d):
        return pltpu.make_async_remote_copy(
            src_ref=cross.at[d],
            dst_ref=cross_in.at[d],
            send_sem=x_send.at[d],
            recv_sem=x_recv.at[d],
            device_id=ahead(1, 0),
            device_id_type=MESH,
        )

    def send_cross(d):
        cross_copy(d).start()

    each(0, half, lambda d: tok_cross(d).wait_recv())
    each(0, half // chunk, lambda c: experts(1, c * chunk))
    each(1, half, send_cross)
    send_cross(0)

    def home_copy(d):
        return pltpu.make_async_remote_copy(
            src_ref=home.at[d],
            dst_ref=home_in.at[d],
            send_sem=h_send.at[d],
            recv_sem=h_recv.at[d],
            device_id=behind(0, d),
            device_id_type=MESH,
        )

    def send_home(d):
        cross_copy(d).wait_recv()
        home[d] = (part[d] + cross_in[d].astype(F32)).astype(BF16)
        home_copy(d).start()

    each(1, half, send_home)
    cross_copy(0).wait_recv()
    part[0] += cross_in[0].astype(F32)

    def collect(d):
        home_copy(d).wait_recv()
        part[0] += home_in[d].astype(F32)

    each(1, half, collect)
    expert_sum = part[0]
    mix_ref[...] = expert_sum.astype(BF16)
    layer_ref[...] = (residual + RESIDUAL * expert_sum).astype(BF16)

    each(1, n_tp, lambda t: tp_copy(t).wait_send())
    each(1, half, lambda d: tok_copy(d).wait_send())
    each(0, half, lambda d: tok_cross(d).wait_send())
    each(0, half, lambda d: cross_copy(d).wait_send())
    each(1, half, lambda d: home_copy(d).wait_send())


def tail(n, n_tp, attended, w_out, hidden, gate_all, expert_in, expert_out):
    half = n // 2
    block, width = hidden.shape
    rows = block // n_tp
    units, ff = expert_out.shape[:2]
    hparts = units * n // EXPERTS
    vmem = pl.BlockSpec(memory_space=pltpu.VMEM)
    hbm = pl.BlockSpec(memory_space=pl.ANY)
    out = jax.ShapeDtypeStruct((rows, width), BF16)
    dma = pltpu.SemaphoreType.DMA
    return pl.pallas_call(
        functools.partial(tail_kernel, n, n_tp, hparts),
        out_shape=(out, out, out),
        in_specs=[vmem, vmem, vmem, vmem, hbm, hbm],
        out_specs=(vmem, vmem, vmem),
        scratch_shapes=[
            pltpu.VMEM(expert_in.shape, BF16),
            pltpu.VMEM(expert_out.shape, BF16),
            pltpu.VMEM((block, width), F32),
            pltpu.VMEM((block, width), BF16),
            pltpu.VMEM((n_tp, rows, width), BF16),
            pltpu.VMEM((2, half, rows, width), BF16),
            pltpu.VMEM((half, rows, width), F32),
            pltpu.VMEM((min(4, half) * rows, width), F32),
            pltpu.VMEM((half, rows, width), BF16),
            pltpu.VMEM((half, rows, width), BF16),
            pltpu.VMEM((half, rows, width), BF16),
            pltpu.VMEM((half, rows, width), BF16),
            dma((2, units)),
            dma((n_tp,)),
            dma((n_tp,)),
            dma((2, half)),
            dma((2, half)),
            dma((half,)),
            dma((half,)),
            dma((half,)),
            dma((half,)),
        ],
        compiler_params=pltpu.CompilerParams(
            collective_id=1,
            has_side_effects=True,
            vmem_limit_bytes=(44 << 20) if half <= 8 else (63 << 20),
        ),
    )(attended, w_out, hidden, gate_all, expert_in, expert_out)


def body(
    hidden_in,
    w_query,
    key_weight,
    value_weight,
    w_out,
    cached_prefix_keys,
    cached_prefix_values,
    doc_ids,
    routes,
    gate_scores,
    expert_in,
    expert_out,
):
    rows_dev = hidden_in.shape[0]
    head_size = HEAD_WIDTH
    kv_width = key_weight.shape[1]
    kv_local = kv_width // head_size
    group_width = w_query.shape[1] // head_size // kv_local
    n, n_tp = lax.axis_size("seq"), lax.axis_size("tp")
    prefix_len = cached_prefix_keys.shape[0] * n
    lanes = jnp.arange(128, dtype=jnp.int32)
    picked = routes[:, :, None] == lanes[None, None, :]
    gates = jnp.sum(jnp.where(picked, gate_scores[:, :, None], 0.0), axis=1)
    kv_all, gate_all = gather(
        n, jnp.concatenate([cached_prefix_keys, cached_prefix_values], axis=1), gates
    )
    kv_all = kv_all.reshape(prefix_len, 2 * kv_width)

    doc_row = doc_ids[0]
    row_index = jnp.arange(rows_dev, dtype=jnp.int32)
    same_doc = doc_row[:, None] == doc_row[None, :]
    doc_start = jnp.min(jnp.where(same_doc, row_index[None, :], rows_dev), axis=1)
    token_positions = (prefix_len + row_index - doc_start).astype(F32)
    normed_input = normalize(hidden_in).astype(BF16)
    query_rows_all = jnp.dot(normed_input, w_query, preferred_element_type=F32).reshape(
        rows_dev, kv_local * group_width, head_size
    )
    query_rows_all = (
        rotary_apply(query_rows_all, token_positions)
        .astype(BF16)
        .reshape(rows_dev, kv_local, group_width, head_size)
    )
    fresh_key = jnp.dot(normed_input, key_weight, preferred_element_type=F32).reshape(
        rows_dev, kv_local, head_size
    )
    fresh_key = rotary_apply(fresh_key, token_positions).astype(BF16)
    fresh_value = (
        jnp.dot(normed_input, value_weight, preferred_element_type=F32)
        .astype(BF16)
        .reshape(rows_dev, kv_local, head_size)
    )
    own_scores = (
        jnp.einsum("tkgd,skd->tkgs", query_rows_all, fresh_key, preferred_element_type=F32)
        / head_size
    )
    visible = same_doc & (row_index[None, :] <= row_index[:, None])
    own_scores = jnp.where(visible[:, None, None, :], own_scores, -jnp.inf)
    key_rows = kv_all[:, :kv_width].reshape(-1, kv_local, head_size)
    value_rows = kv_all[:, kv_width:].reshape(-1, kv_local, head_size)
    scores = (
        jnp.einsum("tkgd,pkd->tkgp", query_rows_all, key_rows, preferred_element_type=F32)
        / head_size
    )
    top = jnp.maximum(jnp.max(own_scores, axis=-1), jnp.max(scores, axis=-1))
    own_weights = jnp.exp(own_scores - top[..., None])
    weights = jnp.exp(scores - top[..., None])
    denominator = jnp.sum(own_weights, axis=-1) + jnp.sum(weights, axis=-1)
    numerator = jnp.einsum(
        "tkgs,skd->tkgd", own_weights.astype(BF16), fresh_value, preferred_element_type=F32
    ) + jnp.einsum("tkgp,pkd->tkgd", weights.astype(BF16), value_rows, preferred_element_type=F32)
    attended = (
        (numerator / denominator[..., None])
        .astype(BF16)
        .reshape(rows_dev, kv_local * group_width * head_size)
    )
    return tail(n, n_tp, attended, w_out, hidden_in, gate_all, expert_in, expert_out)


def solution(mesh):
    in_specs = (
        P("seq", None),
        P(None, "tp"),
        P(None, "tp"),
        P(None, "tp"),
        P("tp", None),
        P("seq", "tp"),
        P("seq", "tp"),
        P("seq", None),
        P(("seq", "tp"), None),
        P(("seq", "tp"), None),
        P("seq", None, None),
        P("seq", None, None),
    )
    out_specs = (P(("seq", "tp"), None), P(("seq", "tp"), None), P(("seq", "tp"), None))
    return jax.shard_map(body, mesh=mesh, in_specs=in_specs, out_specs=out_specs, check_vma=False)
```

time: 218 us -> 70.4 us (0.32)
  blocking collectives: 105 us -> 0 us
  waiting for transfers between devices: 68.9 us -> 0 us
  Pallas kernels: 0 us -> 54.2 us
  between operations: 14.4 us -> 0.84 us
  matrix products: 16.9 us -> 3.46 us
  local copies, waits for them, and re-layouts: 3.43 us -> 7.34 us
  starting transfers between devices: 3.75 us -> 0 us
    all_gather x2 -> x0, blocking collectives: 62.8 us -> none  [the longest x1 32.3 us: body(): lax.all_gather(cached_prefix_keys, 'seq', axis=0, tiled=True)]
    pallas_call x0 -> x2, Pallas kernels: none -> 54.2 us  [the longest x1 41.6 us: tail(): pl.pallas_call(functools.partial(tail_kernel, n, n_tp, hparts), out_shape...]
    all_to_all x1 -> x0, blocking collectives: 41.8 us -> none  [body(): lax.all_to_all(outgoing, 'seq', split_axis=0, concat_axis=0, tiled=True)]
    all_to_all x1 -> x0, waiting for transfers between devices: 34.6 us -> none  [body(): lax.all_to_all(partial_value, 'seq', split_axis=0, concat_axis=0, tiled=T...]
    psum x1 -> x0, waiting for transfers between devices: 34.3 us -> none  [body(): lax.psum(jnp.dot(attended, w_out, preferred_element_type=jnp.float32), 'tp')]
    dot_general x10 -> x5, matrix products: 16.2 us -> 2.86 us  [the longest x1 1.46 us: body(): jnp.dot(normed_input, value_weight, preferred_element_type=F32).astype(BF16)]
    unnamed x22 -> x15, local copies, waits for them, and re-layouts: 0.21 us -> 6.99 us
    all_to_all x1 -> x0, starting transfers between devices: 3.71 us -> none  [body(): lax.all_to_all(partial_value, 'seq', split_axis=0, concat_axis=0, tiled=T...]
  transfers between devices with their start and end apart: 2 -> 0, of which waited for: 2 -> 0; matrix products, arithmetic and copies ran while one was open for 1% -> 0% of each run, Pallas kernels for 0% -> 0%
where the time goes in v2:
time: 70.4 us; the launch traced here: 70 us
  Pallas kernels  54.2 us (77%)
  local copies, waits for them, and re-layouts  7.34 us (10%)
  other arithmetic  4.17 us (6%)
  matrix products  3.46 us (5%)
  between operations  0.84 us (1%)
    pallas_call x1, Pallas kernels, tail(): pl.pallas_call(functools.partial(tail_kernel, n, n_tp, hparts), out_shape...  41.6 us
    pallas_call x1, Pallas kernels, gather(): pl.pallas_call(functools.partial(gather_kernel, n), out_shape=(jax.ShapeD...  12.6 us
    unnamed x15, local copies, waits for them, and re-layouts  6.99 us
    dot_general x1, matrix products, body(): jnp.dot(normed_input, value_weight, preferred_element_type=F32).astype(BF16)  1.46 us

profile of v2, /device:TPU:0, one launch (start us, length us, event | category | flops | bytes accessed | tf_op | source)
XLA Modules:
  0.0 70.0 jit_solution(15484891432944273277)
XLA Ops:
  0.6 0.0 copy-start
  0.6 0.0 copy-start.1
  0.7 0.0 copy-start.4
  0.7 0.9 %fusion.17 = s32[128]{0:T(128)S(1)} fusion(s32[128]{0:T(128)} %bitcast.58), kind=kLoop, calls=%fused_computation.30 | loop fusion | flops 49024 | bytes 1024 | tf_op jit(solution)/shard_map/reduce_min | solution.py:378
  1.6 1.2 %fusion.6 = f32[128]{0:T(128)S(1)} fusion(bf16[128,1536]{1,0:T(8,128)(2,1)} %hidden.1), kind=kLoop, calls=%fused_computation.12 | loop fusion | flops 589696 | bytes 393728 | tf_op jit(solution)/shard_map/reduce_sum | solution.py:21
  2.8 0.7 %pad_maximum_fusion.3.kv_ref = bf16[32,256]{1,0:T(8,128)(2,1)S(1)} fusion(bf16[32,128]{1,0:T(8,128)(2,1)} %param.18, bf16[32,128]{1,0:T(8,128)(2,1)} %param.17), kind=kLoop, calls=%fused_computation.39 | loop fusion | flops 32768 | bytes 32768 | tf_op jit(solution)/shard_map/concatenate | solution.py:371
  3.5 0.8 %compare_and_fusion = pred[128,128]{0,1:T(8,128)(4,1)S(1)} fusion(s32[128]{0:T(128)} %bitcast.59), kind=kLoop, calls=%fused_computation.29 | loop fusion | flops 49152 | bytes 16896 | tf_op jit(solution)/shard_map/and | solution.py:402
  4.3 0.8 %copy.35 = s32[32,8]{1,0:T(8,128)S(1)} copy(s32[32,8]{0,1:T(8,128)} %param.20) | data formatting | bytes 2048 | tf_op args[8]
  5.1 0.8 %copy.36 = f32[32,8]{1,0:T(8,128)S(1)} copy(f32[32,8]{0,1:T(8,128)} %param.21) | data formatting | bytes 2048 | tf_op args[9]
  5.8 0.1 select_reduce_fusion.gate_ref
  6.0 0.1 multiply_cosine_fusion
  6.1 1.5 %convolution_convert_fusion = bf16[128,128]{0,1:T(8,128)(2,1)S(1)} fusion(bf16[1536,128]{1,0:T(8,128)(2,1)} %param.15, bf16[128,1536]{1,0:T(8,128)(2,1)} %hidden.1, f32[128]{0:T(128)S(1)} %add_rsqrt_fusion), kind=kOutput, calls=%fused_computation.9 | convolution fusion | flops 50937856 | bytes 819712 | tf_op jit(solution)/shard_map/dot_general | solution.py:394
  7.6 0.0 copy-done.1
  7.6 0.0 copy-done.4
  7.6 0.4 fusion.24
  8.0 0.0 copy-done
  8.0 0.6 fusion.22
  8.7 12.6 %shard_map.139 = (bf16[2,4,32,256]{3,2,1,0:T(8,128)(2,1)S(1)}, f32[2,4,32,128]{3,2,1,0:T(8,128)S(1)}) custom-call(bf16[32,256]{1,0:T(8,128)(2,1)S(1)} %pad_maximum_fusion.3.kv_ref, f32[32,128]{1,0:T(8,128)S(1)} %select_reduce_fusion.gate_ref), custom_call_target="tpu_custom_call" | custom-call | tf_op jit(solution)/shard_map/pallas_call | solution.py:114
  21.3 0.1 copy.39
  21.4 0.1 copy.37
  21.5 0.3 fusion.28
  21.8 0.3 fusion.29
  22.1 0.1 fusion.12
  22.2 0.2 fusion.14
  22.4 0.0 copy-start.3
  22.4 0.1 fusion.8
  22.5 0.3 fusion.5
  22.8 0.1 copy.41.attended
  22.9 0.7 %copy-done.3 = bf16[384,1536]{1,0:T(8,128)(2,1)S(1)} copy-done((bf16[384,1536]{1,0:T(8,128)(2,1)S(1)}, bf16[384,1536]{1,0:T(8,128)(2,1)}, u32[]{:S(2)}) %copy-start.3) | copy-done | bytes 1179672
  23.7 0.0 copy-start.2
  23.7 2.8 %copy-done.2 = bf16[4,512,1536]{2,1,0:T(8,128)(2,1)S(1)} copy-done((bf16[4,512,1536]{2,1,0:T(8,128)(2,1)S(1)}, bf16[4,512,1536]{2,1,0:T(8,128)(2,1)}, u32[]{:S(2)}) %copy-start.2) | copy-done | bytes 6291480
  26.4 41.6 %shard_map.140 = (bf16[32,1536]{1,0:T(8,128)(2,1)S(1)}, bf16[32,1536]{1,0:T(8,128)(2,1)S(1)}, bf16[32,1536]{1,0:T(8,128)(2,1)S(1)}) custom-call(bf16[128,384]{1,0:T(8,128)(2,1)S(1)} %copy.41.attended, bf16[384,1536]{1,0:T(8,128)(2,1)S(1)} %copy-done.3, bf16[128,1536]{1,0:T(8,128)(2,1)S(1)} %copy-done.1, f32[2,4,32,128]{3,2,1,0:T(8,128)S(1)} %get-tuple-element.6.gate_all, ...), custom_call_target="tpu_custom_call" | custom-call | tf_op jit(solution)/shard_map/pallas_call | solution.py:310
  68.1 0.6 copy.52
  68.7 0.6 copy.53
  69.4 0.6 copy.54
  (8 shorter events, 0.1 us)
Async XLA Ops:
  0.6 7.4 %copy-start = (bf16[1536,384]{1,0:T(8,128)(2,1)S(1)}, bf16[1536,384]{1,0:T(8,128)(2,1)}, u32[]{:S(2)}) copy-start(bf16[1536,384]{1,0:T(8,128)(2,1)} %param.13) | copy-start | bytes 3538948
  0.6 7.0 %copy-start.1 = (bf16[128,1536]{1,0:T(8,128)(2,1)S(1)}, bf16[128,1536]{1,0:T(8,128)(2,1)}, u32[]{:S(2)}) copy-start(bf16[128,1536]{1,0:T(8,128)(2,1)} %hidden.1) | copy-start | bytes 1179652
  0.7 7.0 %copy-start.4 = (bf16[1536,128]{1,0:T(8,128)(2,1)S(1)}, bf16[1536,128]{1,0:T(8,128)(2,1)}, u32[]{:S(2)}) copy-start(bf16[1536,128]{1,0:T(8,128)(2,1)} %param.14) | copy-start | bytes 1179652
  22.4 1.3 %copy-start.3 = (bf16[384,1536]{1,0:T(8,128)(2,1)S(1)}, bf16[384,1536]{1,0:T(8,128)(2,1)}, u32[]{:S(2)}) copy-start(bf16[384,1536]{1,0:T(8,128)(2,1)} %w_out.1) | copy-start | bytes 3538948
  23.7 2.8 %copy-start.2 = (bf16[4,512,1536]{2,1,0:T(8,128)(2,1)S(1)}, bf16[4,512,1536]{2,1,0:T(8,128)(2,1)}, u32[]{:S(2)}) copy-start(bf16[4,512,1536]{2,1,0:T(8,128)(2,1)} %out_hbm.1) | copy-start | bytes 18874372

commit v3 on v2

--- a/solution.py
+++ b/solution.py
@@ -21,22 +21,6 @@
     return values * lax.rsqrt(jnp.mean(values * values, axis=-1, keepdims=True) + EPSILON)
 
 
-def rotary_apply(values, token_positions):
-    half_size = values.shape[-1] // 2
-    frequency = jnp.exp(
-        -jnp.log(10000.0) * jnp.arange(half_size, dtype=F32) * 2.0 / values.shape[-1]
-    )
-    angles = token_positions[:, None] * frequency[None, :]
-    cosine = jnp.cos(angles)[:, None, :]
-    sine_part = jnp.sin(angles)[:, None, :]
-    first_half = values[..., :half_size]
-    second = values[..., half_size:]
-    return jnp.concatenate(
-        [first_half * cosine - second * sine_part, second * cosine + first_half * sine_part],
-        axis=-1,
-    )
-
-
 def each(start, stop, fn):
     if stop - start <= 8:
         for i in range(start, stop):
@@ -64,12 +48,25 @@
     return half, ahead, behind
 
 
-def gather_kernel(n, kv_ref, gate_ref, kv_all, gate_all, send, recv, local):
+def attend_kernel(
+    n,
+    hidden, key_own, value_own, docs, routes, scores, wq_hbm, wk_hbm, wv_hbm,
+    attended, gate_all,
+    wq, wk, wv, packed, key_all, value_all, gates_in, w_sem, send, recv,
+):
     half, ahead, _ = peers(n)
-    own_a = pltpu.make_async_copy(kv_ref, kv_all.at[0, 0], local.at[0])
-    own_b = pltpu.make_async_copy(gate_ref, gate_all.at[0, 0], local.at[1])
-    own_a.start()
-    own_b.start()
+    block = hidden.shape[0]
+    rows = routes.shape[0]
+    share = key_own.shape[0]
+    head_size = HEAD_WIDTH
+    kv_local = wk.shape[1] // head_size
+    group = wq.shape[1] // wk.shape[1]
+    fetches = [
+        pltpu.make_async_copy(src, dst, w_sem.at[i])
+        for i, (src, dst) in enumerate(((wq_hbm, wq), (wk_hbm, wk), (wv_hbm, wv)))
+    ]
+    for f in fetches:
+        f.start()
     barrier = pltpu.get_barrier_semaphore()
 
     def greet(side, step):
@@ -77,19 +74,33 @@
 
     each(1, half, lambda step: greet(0, step))
     each(0, half, lambda step: greet(1, step))
+
+    lanes_g = lax.broadcasted_iota(jnp.int32, (rows, 128), 1)
+    dense = jnp.zeros((rows, 128), F32)
+    for k in range(routes.shape[1]):
+        dense = dense + jnp.where(lanes_g == routes[:, k : k + 1], scores[:, k : k + 1], 0.0)
+    tile = dense[0:8]
+    for i in range(1, rows // 8):
+        tile = tile + pltpu.roll(dense[8 * i : 8 * i + 8], 32 * i, 1)
+    packed[...] = tile
+    gates_in[0] = tile
+    key_all[0] = key_own[...]
+    value_all[0] = value_own[...]
     pl.semaphore_wait(barrier, n - 1)
 
     def copies(side, step):
+        slot = side * half + step
+        pairs = ((key_own, key_all), (value_own, value_all), (packed, gates_in))
         return [
             pltpu.make_async_remote_copy(
                 src_ref=src,
-                dst_ref=dst.at[side, step],
-                send_sem=send.at[kind, side, step],
-                recv_sem=recv.at[kind, side, step],
+                dst_ref=dst.at[slot],
+                send_sem=send.at[kind, slot],
+                recv_sem=recv.at[kind, slot],
                 device_id=ahead(side, step),
                 device_id_type=MESH,
             )
-            for kind, (src, dst) in enumerate(((kv_ref, kv_all), (gate_ref, gate_all)))
+            for kind, (src, dst) in enumerate(pairs)
         ]
 
     def start(side, step):
@@ -102,40 +113,139 @@
 
     each(1, half, lambda step: start(0, step))
     each(0, half, lambda step: start(1, step))
+
+    normed = normalize(hidden[...]).astype(BF16)
+    doc = jnp.broadcast_to(docs[...].astype(F32), (block, block))
+    lane = lax.broadcasted_iota(jnp.int32, (block, block), 1)
+    row = lax.broadcasted_iota(jnp.int32, (block, block), 0)
+    same = doc == doc.T
+    first = jnp.min(jnp.where(same, lane, block).astype(F32), axis=1, keepdims=True)
+    positions = (share * n + row).astype(F32) - first
+    pair = lax.broadcasted_iota(jnp.int32, (block, 128), 1)
+    low_half = lax.rem(pair, head_size) < head_size // 2
+    place = lax.rem(pair, head_size // 2).astype(F32)
+    frequency = jnp.exp(-jnp.log(jnp.float32(10000.0)) * place * 2.0 / head_size)
+    angles = positions[:, :1] * frequency
+    cosine = jnp.cos(angles)
+    sine = jnp.sin(angles)
+    sine = jnp.where(low_half, -sine, sine)
+
+    def rope(x):
+        turned = jnp.where(
+            low_half,
+            pltpu.roll(x, 128 - head_size // 2, 1),
+            pltpu.roll(x, head_size // 2, 1),
+        )
+        return (x * cosine + turned * sine).astype(BF16)
+
+    def heads(x):
+        return [x[:, j * head_size : (j + 1) * head_size] for j in range(128 // head_size)]
+
+    def roped_heads(x):
+        return [h for j in range(x.shape[1] // 128) for h in heads(rope(x[:, j * 128 : j * 128 + 128]))]
+
+    for f in fetches:
+        f.wait()
+    q = roped_heads(jnp.dot(normed, wq[...], preferred_element_type=F32))
+    k = roped_heads(jnp.dot(normed, wk[...], preferred_element_type=F32))
+    v = jnp.dot(normed, wv[...], preferred_element_type=F32).astype(BF16)
+    v = [v[:, j * head_size : (j + 1) * head_size] for j in range(kv_local)]
+    visible = same & (lane <= row)
+    visible = jnp.concatenate([visible.astype(F32)] * group, axis=0) > 0.5
+    contract = (((1,), (1,)), ((), ()))
+    states = []
+    queries = []
+    for g in range(kv_local):
+        query = jnp.concatenate(q[g * group : (g + 1) * group], axis=0)
+        own = lax.dot_general(query, k[g], contract, preferred_element_type=F32) / head_size
+        own = jnp.where(visible, own, -jnp.inf)
+        top = jnp.max(own, axis=1, keepdims=True)
+        weights = jnp.exp(own - top)
+        total = jnp.sum(weights, axis=1, keepdims=True)
+        mixed = jnp.dot(weights.astype(BF16), v[g], preferred_element_type=F32)
+        queries.append(query)
+        states += [top, total, mixed]
+
     each(1, half, lambda step: finish(0, step))
     each(0, half, lambda step: finish(1, step))
-    own_a.wait()
-    own_b.wait()
-
-
-def gather(n, kv, gates):
-    half = n // 2
+
+    span = 8 if n % 8 == 0 else n
+
+    def prefix(begin, carry):
+        keys = key_all[pl.ds(begin, span)].reshape(span * share, kv_local * head_size)
+        values = value_all[pl.ds(begin, span)].reshape(span * share, kv_local * head_size)
+        out = []
+        for g in range(kv_local):
+            top, total, mixed = carry[3 * g : 3 * g + 3]
+            mine = slice(g * head_size, (g + 1) * head_size)
+            sc = lax.dot_general(queries[g], keys[:, mine], contract, preferred_element_type=F32)
+            sc = sc / head_size
+            higher = jnp.maximum(top, jnp.max(sc, axis=1, keepdims=True))
+            shrink = jnp.exp(top - higher)
+            weights = jnp.exp(sc - higher)
+            total = total * shrink + jnp.sum(weights, axis=1, keepdims=True)
+            mixed = mixed * shrink + jnp.dot(
+                weights.astype(BF16), values[:, mine], preferred_element_type=F32
+            )
+            out += [higher, total, mixed]
+        return tuple(out)
+
+    if n == span:
+        states = prefix(0, tuple(states))
+    else:
+        states = lax.fori_loop(0, n // span, lambda c, s: prefix(c * span, s), tuple(states))
+    done = []
+    for g in range(kv_local):
+        _, total, mixed = states[3 * g : 3 * g + 3]
+        result = mixed / total
+        done += [result[j * block : (j + 1) * block] for j in range(group)]
+    attended[...] = jnp.concatenate(done, axis=1).astype(BF16)
+
+    def unpack(slot):
+        t = gates_in[slot]
+        gate_all[slot, 0:8] = t
+        for i in range(1, rows // 8):
+            gate_all[slot, 8 * i : 8 * i + 8] = pltpu.roll(t, 128 - 32 * i, 1)
+
+    each(0, n, unpack)
+
+
+def attend(n, hidden, key_own, value_own, docs, routes, scores, w_query, key_weight, value_weight):
     vmem = pl.BlockSpec(memory_space=pltpu.VMEM)
+    hbm = pl.BlockSpec(memory_space=pl.ANY)
+    rows = routes.shape[0]
     return pl.pallas_call(
-        functools.partial(gather_kernel, n),
+        functools.partial(attend_kernel, n),
         out_shape=(
-            jax.ShapeDtypeStruct((2, half) + kv.shape, kv.dtype),
-            jax.ShapeDtypeStruct((2, half) + gates.shape, gates.dtype),
+            jax.ShapeDtypeStruct((hidden.shape[0], w_query.shape[1]), BF16),
+            jax.ShapeDtypeStruct((n, rows, 128), F32),
         ),
-        in_specs=[vmem, vmem],
+        in_specs=[vmem] * 6 + [hbm] * 3,
         out_specs=(vmem, vmem),
         scratch_shapes=[
-            pltpu.SemaphoreType.DMA((2, 2, half)),
-            pltpu.SemaphoreType.DMA((2, 2, half)),
-            pltpu.SemaphoreType.DMA((2,)),
+            pltpu.VMEM(w_query.shape, BF16),
+            pltpu.VMEM(key_weight.shape, BF16),
+            pltpu.VMEM(value_weight.shape, BF16),
+            pltpu.VMEM((8, 128), F32),
+            pltpu.VMEM((n,) + key_own.shape, BF16),
+            pltpu.VMEM((n,) + value_own.shape, BF16),
+            pltpu.VMEM((n, 8, 128), F32),
+            pltpu.SemaphoreType.DMA((3,)),
+            pltpu.SemaphoreType.DMA((3, n)),
+            pltpu.SemaphoreType.DMA((3, n)),
         ],
         compiler_params=pltpu.CompilerParams(
-            collective_id=0, has_side_effects=True, vmem_limit_bytes=32 << 20
+            collective_id=0, has_side_effects=True, vmem_limit_bytes=40 << 20
         ),
-    )(kv, gates)
+    )(hidden, key_own, value_own, docs, routes, scores, w_query, key_weight, value_weight)
 
 
 def tail_kernel(
     n, n_tp, hparts,
-    attended, w_out, hidden, gate_all, in_hbm, out_hbm,
+    attended, hidden, gate_all, w_out_hbm, in_hbm, out_hbm,
     proj_ref, mix_ref, layer_ref,
-    w_in, w_back, sums, outbox, inbox, tok, part, acc, cross, cross_in, home, home_in,
-    w_sem, tp_send, tp_recv, tok_send, tok_recv, x_send, x_recv, h_send, h_recv,
+    w_out, w_in, w_back, sums, outbox, inbox, tok, part, acc, cross, cross_in, home, home_in,
+    o_sem, w_sem, tp_send, tp_recv, tok_send, tok_recv, x_send, x_recv, h_send, h_recv,
 ):
     half, ahead, behind = peers(n)
     units, ff = out_hbm.shape[0], out_hbm.shape[1]
@@ -149,6 +259,8 @@
             pltpu.make_async_copy(out_hbm.at[u], w_back.at[u], w_sem.at[1, u]),
         )
 
+    out_fetch = pltpu.make_async_copy(w_out_hbm, w_out, o_sem)
+    out_fetch.start()
     barrier = pltpu.get_barrier_semaphore()
 
     def greet(where):
@@ -163,6 +275,7 @@
     for u in range(units):
         for c in fetch(u):
             c.start()
+    out_fetch.wait()
     whole = jnp.dot(attended[...], w_out[...], preferred_element_type=F32)
     sums[...] = whole
     outbox[...] = whole.astype(BF16)
@@ -223,7 +336,7 @@
 
     def experts(side, begin):
         tokens = tok[side, pl.ds(begin, chunk)].reshape(chunk * rows, width)
-        gates = gate_all[side, pl.ds(begin, chunk)].reshape(chunk * rows, gate_all.shape[-1])
+        gates = gate_all[pl.ds(side * half + begin, chunk)].reshape(chunk * rows, gate_all.shape[-1])
         lanes = lax.broadcasted_iota(jnp.int32, gates.shape, 1)
         acc[...] = jnp.zeros(acc.shape, F32)
 
@@ -310,9 +423,10 @@
     return pl.pallas_call(
         functools.partial(tail_kernel, n, n_tp, hparts),
         out_shape=(out, out, out),
-        in_specs=[vmem, vmem, vmem, vmem, hbm, hbm],
+        in_specs=[vmem, vmem, vmem, hbm, hbm, hbm],
         out_specs=(vmem, vmem, vmem),
         scratch_shapes=[
+            pltpu.VMEM(w_out.shape, BF16),
             pltpu.VMEM(expert_in.shape, BF16),
             pltpu.VMEM(expert_out.shape, BF16),
             pltpu.VMEM((block, width), F32),
@@ -325,6 +439,7 @@
             pltpu.VMEM((half, rows, width), BF16),
             pltpu.VMEM((half, rows, width), BF16),
             pltpu.VMEM((half, rows, width), BF16),
+            dma,
             dma((2, units)),
             dma((n_tp,)),
             dma((n_tp,)),
@@ -340,7 +455,7 @@
             has_side_effects=True,
             vmem_limit_bytes=(44 << 20) if half <= 8 else (63 << 20),
         ),
-    )(attended, w_out, hidden, gate_all, expert_in, expert_out)
+    )(attended, hidden, gate_all, w_out, expert_in, expert_out)
 
 
 def body(
@@ -357,67 +472,10 @@
     expert_in,
     expert_out,
 ):
-    rows_dev = hidden_in.shape[0]
-    head_size = HEAD_WIDTH
-    kv_width = key_weight.shape[1]
-    kv_local = kv_width // head_size
-    group_width = w_query.shape[1] // head_size // kv_local
     n, n_tp = lax.axis_size("seq"), lax.axis_size("tp")
-    prefix_len = cached_prefix_keys.shape[0] * n
-    lanes = jnp.arange(128, dtype=jnp.int32)
-    picked = routes[:, :, None] == lanes[None, None, :]
-    gates = jnp.sum(jnp.where(picked, gate_scores[:, :, None], 0.0), axis=1)
-    kv_all, gate_all = gather(
-        n, jnp.concatenate([cached_prefix_keys, cached_prefix_values], axis=1), gates
-    )
-    kv_all = kv_all.reshape(prefix_len, 2 * kv_width)
-
-    doc_row = doc_ids[0]
-    row_index = jnp.arange(rows_dev, dtype=jnp.int32)
-    same_doc = doc_row[:, None] == doc_row[None, :]
-    doc_start = jnp.min(jnp.where(same_doc, row_index[None, :], rows_dev), axis=1)
-    token_positions = (prefix_len + row_index - doc_start).astype(F32)
-    normed_input = normalize(hidden_in).astype(BF16)
-    query_rows_all = jnp.dot(normed_input, w_query, preferred_element_type=F32).reshape(
-        rows_dev, kv_local * group_width, head_size
-    )
-    query_rows_all = (
-        rotary_apply(query_rows_all, token_positions)
-        .astype(BF16)
-        .reshape(rows_dev, kv_local, group_width, head_size)
-    )
-    fresh_key = jnp.dot(normed_input, key_weight, preferred_element_type=F32).reshape(
-        rows_dev, kv_local, head_size
-    )
-    fresh_key = rotary_apply(fresh_key, token_positions).astype(BF16)
-    fresh_value = (
-        jnp.dot(normed_input, value_weight, preferred_element_type=F32)
-        .astype(BF16)
-        .reshape(rows_dev, kv_local, head_size)
-    )
-    own_scores = (
-        jnp.einsum("tkgd,skd->tkgs", query_rows_all, fresh_key, preferred_element_type=F32)
-        / head_size
-    )
-    visible = same_doc & (row_index[None, :] <= row_index[:, None])
-    own_scores = jnp.where(visible[:, None, None, :], own_scores, -jnp.inf)
-    key_rows = kv_all[:, :kv_width].reshape(-1, kv_local, head_size)
-    value_rows = kv_all[:, kv_width:].reshape(-1, kv_local, head_size)
-    scores = (
-        jnp.einsum("tkgd,pkd->tkgp", query_rows_all, key_rows, preferred_element_type=F32)
-        / head_size
-    )
-    top = jnp.maximum(jnp.max(own_scores, axis=-1), jnp.max(scores, axis=-1))
-    own_weights = jnp.exp(own_scores - top[..., None])
-    weights = jnp.exp(scores - top[..., None])
-    denominator = jnp.sum(own_weights, axis=-1) + jnp.sum(weights, axis=-1)
-    numerator = jnp.einsum(
-        "tkgs,skd->tkgd", own_weights.astype(BF16), fresh_value, preferred_element_type=F32
-    ) + jnp.einsum("tkgp,pkd->tkgd", weights.astype(BF16), value_rows, preferred_element_type=F32)
-    attended = (
-        (numerator / denominator[..., None])
-        .astype(BF16)
-        .reshape(rows_dev, kv_local * group_width * head_size)
+    attended, gate_all = attend(
+        n, hidden_in, cached_prefix_keys, cached_prefix_values, doc_ids, routes, gate_scores,
+        w_query, key_weight, value_weight,
     )
     return tail(n, n_tp, attended, w_out, hidden_in, gate_all, expert_in, expert_out)
 

time: 70.4 us -> 70 us (level)
  local copies, waits for them, and re-layouts: 7.34 us -> 14.8 us
  other arithmetic: 4.17 us -> 0 us
  matrix products: 3.46 us -> 0 us
    unnamed x15 -> x25, local copies, waits for them, and re-layouts: 6.99 us -> 14.8 us
    dot_general x7 -> x0, matrix products: 3.46 us -> none  [the longest x1 1.46 us: body(): jnp.dot(normed_input, value_weight, preferred_element_type=F32).astype(BF16)]
    reduce_sum x4 -> x0, other arithmetic: 1.5 us -> none  [the longest x1 1.16 us: normalize(): jnp.mean(values * values, axis=-1, keepdims=True) + EPSILON]
    reduce_min x1 -> x0, other arithmetic: 0.9 us -> none  [body(): jnp.min(jnp.where(same_doc, row_index[None, :], rows_dev), axis=1)]
    and x1 -> x0, other arithmetic: 0.81 us -> none  [body(): visible = same_doc & (row_index[None, :] <= row_index[:, None])]
    concatenate x1 -> x0, other arithmetic: 0.73 us -> none  [body(): jnp.concatenate([cached_prefix_keys, cached_prefix_values], axis=1)]
where the time goes in v3:
time: 70 us; the launch traced here: 69.4 us
  Pallas kernels  54 us (77%)
  local copies, waits for them, and re-layouts  14.8 us (21%)
    pallas_call x1, Pallas kernels, tail(): pl.pallas_call(functools.partial(tail_kernel, n, n_tp, hparts), out_shape...  42 us
    unnamed x25, local copies, waits for them, and re-layouts  14.8 us
    pallas_call x1, Pallas kernels, attend(): pl.pallas_call(functools.partial(attend_kernel, n), out_shape=(jax.ShapeD...  12 us

profile of v3, /device:TPU:0, one launch (start us, length us, event | category | flops | bytes accessed | tf_op | source)
XLA Modules:
  0.0 69.4 jit_solution(5536651201801677269)
XLA Ops:
  0.6 0.8 %copy.15.routes = s32[32,8]{1,0:T(8,128)S(1)} copy(s32[32,8]{0,1:T(8,128)} %param.20) | data formatting | bytes 2048 | tf_op args[8]
  1.4 0.8 %copy.16.scores = f32[32,8]{1,0:T(8,128)S(1)} copy(f32[32,8]{0,1:T(8,128)} %param.21) | data formatting | bytes 2048 | tf_op args[9]
  2.2 0.0 copy-start.1
  2.2 1.0 %copy-done.1 = bf16[128,1536]{1,0:T(8,128)(2,1)S(1)} copy-done((bf16[128,1536]{1,0:T(8,128)(2,1)S(1)}, bf16[128,1536]{1,0:T(8,128)(2,1)}, u32[]{:S(2)}) %copy-start.1) | copy-done | bytes 393240
  3.2 0.0 copy-start.4
  3.2 1.3 %copy-done.4 = bf16[1536,384]{1,0:T(8,128)(2,1)S(1)} copy-done((bf16[1536,384]{1,0:T(8,128)(2,1)S(1)}, bf16[1536,384]{1,0:T(8,128)(2,1)}, u32[]{:S(2)}) %copy-start.4) | copy-done | bytes 1179672
  4.4 0.0 copy-start.5
  4.4 1.0 %copy-done.5 = bf16[1536,128]{1,0:T(8,128)(2,1)S(1)} copy-done((bf16[1536,128]{1,0:T(8,128)(2,1)S(1)}, bf16[1536,128]{1,0:T(8,128)(2,1)}, u32[]{:S(2)}) %copy-start.5) | copy-done | bytes 393240
  5.4 0.0 copy-start.6
  5.4 1.0 %copy-done.6 = bf16[1536,128]{1,0:T(8,128)(2,1)S(1)} copy-done((bf16[1536,128]{1,0:T(8,128)(2,1)S(1)}, bf16[1536,128]{1,0:T(8,128)(2,1)}, u32[]{:S(2)}) %copy-start.6) | copy-done | bytes 393240
  6.4 0.0 copy-start.7
  6.4 0.7 %copy-done.7 = bf16[32,128]{1,0:T(8,128)(2,1)S(1)} copy-done((bf16[32,128]{1,0:T(8,128)(2,1)S(1)}, bf16[32,128]{1,0:T(8,128)(2,1)}, u32[]{:S(2)}) %copy-start.7) | copy-done | bytes 8216
  7.1 0.0 copy-start.8
  7.1 0.7 %copy-done.8 = bf16[32,128]{1,0:T(8,128)(2,1)S(1)} copy-done((bf16[32,128]{1,0:T(8,128)(2,1)S(1)}, bf16[32,128]{1,0:T(8,128)(2,1)}, u32[]{:S(2)}) %copy-start.8) | copy-done | bytes 8216
  7.8 0.0 copy-start.9
  7.8 0.7 copy-done.9
  8.5 12.0 %shard_map.139 = (bf16[128,384]{1,0:T(8,128)(2,1)S(1)}, f32[8,32,128]{2,1,0:T(8,128)S(1)}) custom-call(bf16[128,1536]{1,0:T(8,128)(2,1)S(1)} %copy-done.1, bf16[32,128]{1,0:T(8,128)(2,1)S(1)} %copy-done.7, bf16[32,128]{1,0:T(8,128)(2,1)S(1)} %copy-done.8, s32[1,128]{1,0:T(1,128)S(1)} %copy-done.9, s32[32,8]{1,0:T(8,128)S(1)} %copy.15.routes, ...), custom_call_target="tpu_custom_call" | custom-call | tf_op jit(solution)/shard_map/pallas_call | solution.py:217
  20.5 0.0 copy-start
  20.5 2.8 %copy-done = bf16[4,512,1536]{2,1,0:T(8,128)(2,1)S(1)} copy-done((bf16[4,512,1536]{2,1,0:T(8,128)(2,1)S(1)}, bf16[4,512,1536]{2,1,0:T(8,128)(2,1)}, u32[]{:S(2)}) %copy-start) | copy-done | bytes 6291480
  23.2 0.0 copy-start.2
  23.2 1.0 %copy-done.2 = bf16[128,1536]{1,0:T(8,128)(2,1)S(1)} copy-done((bf16[128,1536]{1,0:T(8,128)(2,1)S(1)}, bf16[128,1536]{1,0:T(8,128)(2,1)}, u32[]{:S(2)}) %copy-start.2) | copy-done | bytes 393240
  24.2 0.0 copy-start.3
  24.2 1.3 %copy-done.3 = bf16[384,1536]{1,0:T(8,128)(2,1)S(1)} copy-done((bf16[384,1536]{1,0:T(8,128)(2,1)S(1)}, bf16[384,1536]{1,0:T(8,128)(2,1)}, u32[]{:S(2)}) %copy-start.3) | copy-done | bytes 1179672
  25.5 42.0 %shard_map.140 = (bf16[32,1536]{1,0:T(8,128)(2,1)S(1)}, bf16[32,1536]{1,0:T(8,128)(2,1)S(1)}, bf16[32,1536]{1,0:T(8,128)(2,1)S(1)}) custom-call(bf16[128,384]{1,0:T(8,128)(2,1)S(1)} %get-tuple-element.5.attended, bf16[128,1536]{1,0:T(8,128)(2,1)S(1)} %copy-done.2, f32[8,32,128]{2,1,0:T(8,128)S(1)} %get-tuple-element.6.gate_all, ...), custom_call_target="tpu_custom_call" | custom-call | tf_op jit(solution)/shard_map/pallas_call | solution.py:423
  67.5 0.6 copy.20
  68.2 0.6 copy.21
  68.8 0.6 copy.22
Async XLA Ops:
  2.2 1.0 %copy-start.1 = (bf16[128,1536]{1,0:T(8,128)(2,1)S(1)}, bf16[128,1536]{1,0:T(8,128)(2,1)}, u32[]{:S(2)}) copy-start(bf16[128,1536]{1,0:T(8,128)(2,1)} %hidden.3) | copy-start | bytes 1179652
  3.2 1.3 %copy-start.4 = (bf16[1536,384]{1,0:T(8,128)(2,1)S(1)}, bf16[1536,384]{1,0:T(8,128)(2,1)}, u32[]{:S(2)}) copy-start(bf16[1536,384]{1,0:T(8,128)(2,1)} %wq_hbm.1) | copy-start | bytes 3538948
  4.4 1.0 %copy-start.5 = (bf16[1536,128]{1,0:T(8,128)(2,1)S(1)}, bf16[1536,128]{1,0:T(8,128)(2,1)}, u32[]{:S(2)}) copy-start(bf16[1536,128]{1,0:T(8,128)(2,1)} %wk_hbm.1) | copy-start | bytes 1179652
  5.4 1.0 %copy-start.6 = (bf16[1536,128]{1,0:T(8,128)(2,1)S(1)}, bf16[1536,128]{1,0:T(8,128)(2,1)}, u32[]{:S(2)}) copy-start(bf16[1536,128]{1,0:T(8,128)(2,1)} %wv_hbm.1) | copy-start | bytes 1179652
  6.4 0.7 %copy-start.7 = (bf16[32,128]{1,0:T(8,128)(2,1)S(1)}, bf16[32,128]{1,0:T(8,128)(2,1)}, u32[]{:S(2)}) copy-start(bf16[32,128]{1,0:T(8,128)(2,1)} %key_own.1) | copy-start | bytes 24580
  7.1 0.7 %copy-start.8 = (bf16[32,128]{1,0:T(8,128)(2,1)S(1)}, bf16[32,128]{1,0:T(8,128)(2,1)}, u32[]{:S(2)}) copy-start(bf16[32,128]{1,0:T(8,128)(2,1)} %value_own.1) | copy-start | bytes 24580
  7.8 0.7 copy-start.9
  20.5 2.8 %copy-start = (bf16[4,512,1536]{2,1,0:T(8,128)(2,1)S(1)}, bf16[4,512,1536]{2,1,0:T(8,128)(2,1)}, u32[]{:S(2)}) copy-start(bf16[4,512,1536]{2,1,0:T(8,128)(2,1)} %out_hbm.1) | copy-start | bytes 18874372
  23.2 1.0 %copy-start.2 = (bf16[128,1536]{1,0:T(8,128)(2,1)S(1)}, bf16[128,1536]{1,0:T(8,128)(2,1)}, u32[]{:S(2)}) copy-start(bf16[128,1536]{1,0:T(8,128)(2,1)} %hidden.3) | copy-start | bytes 1179652
  24.2 1.3 %copy-start.3 = (bf16[384,1536]{1,0:T(8,128)(2,1)S(1)}, bf16[384,1536]{1,0:T(8,128)(2,1)}, u32[]{:S(2)}) copy-start(bf16[384,1536]{1,0:T(8,128)(2,1)} %w_out_hbm.1) | copy-start | bytes 3538948

commit v4 on v3

--- a/solution.py
+++ b/solution.py
@@ -212,7 +212,7 @@
 
 def attend(n, hidden, key_own, value_own, docs, routes, scores, w_query, key_weight, value_weight):
     vmem = pl.BlockSpec(memory_space=pltpu.VMEM)
-    hbm = pl.BlockSpec(memory_space=pl.ANY)
+    hbm = pl.BlockSpec(memory_space=pltpu.HBM)
     rows = routes.shape[0]
     return pl.pallas_call(
         functools.partial(attend_kernel, n),
@@ -235,7 +235,7 @@
             pltpu.SemaphoreType.DMA((3, n)),
         ],
         compiler_params=pltpu.CompilerParams(
-            collective_id=0, has_side_effects=True, vmem_limit_bytes=40 << 20
+            collective_id=0, has_side_effects=True, vmem_limit_bytes=60 << 20
         ),
     )(hidden, key_own, value_own, docs, routes, scores, w_query, key_weight, value_weight)
 
@@ -417,7 +417,7 @@
     units, ff = expert_out.shape[:2]
     hparts = units * n // EXPERTS
     vmem = pl.BlockSpec(memory_space=pltpu.VMEM)
-    hbm = pl.BlockSpec(memory_space=pl.ANY)
+    hbm = pl.BlockSpec(memory_space=pltpu.HBM)
     out = jax.ShapeDtypeStruct((rows, width), BF16)
     dma = pltpu.SemaphoreType.DMA
     return pl.pallas_call(
@@ -453,7 +453,7 @@
         compiler_params=pltpu.CompilerParams(
             collective_id=1,
             has_side_effects=True,
-            vmem_limit_bytes=(44 << 20) if half <= 8 else (63 << 20),
+            vmem_limit_bytes=62 << 20,
         ),
     )(attended, hidden, gate_all, w_out, expert_in, expert_out)
 

time: 70 us -> 65 us (0.929)
  local copies, waits for them, and re-layouts: 14.8 us -> 7.35 us
  Pallas kernels: 54 us -> 56.7 us
    unnamed x25 -> x5, local copies, waits for them, and re-layouts: 14.8 us -> 7.35 us
    pallas_call x1, Pallas kernels: 42 us -> 43.7 us  [tail(): pl.pallas_call(functools.partial(tail_kernel, n, n_tp, hparts), out_shape...]
    pallas_call x1, Pallas kernels: 12 us -> 13.1 us  [attend(): pl.pallas_call(functools.partial(attend_kernel, n), out_shape=(jax.ShapeD...]
where the time goes in v4:
time: 65 us; the launch traced here: 64.7 us
  Pallas kernels  56.7 us (87%)
  local copies, waits for them, and re-layouts  7.35 us (11%)
  between operations  0.65 us (1%)
    pallas_call x1, Pallas kernels, tail(): pl.pallas_call(functools.partial(tail_kernel, n, n_tp, hparts), out_shape...  43.7 us
    pallas_call x1, Pallas kernels, attend(): pl.pallas_call(functools.partial(attend_kernel, n), out_shape=(jax.ShapeD...  13.1 us
    unnamed x5, local copies, waits for them, and re-layouts  7.35 us

profile of v4, /device:TPU:0, one launch (start us, length us, event | category | flops | bytes accessed | tf_op | source)
XLA Modules:
  0.0 64.7 jit_solution(5234339891443328391)
XLA Ops:
  0.6 1.4 %copy.15.routes = s32[32,8]{1,0:T(8,128)} copy(s32[32,8]{0,1:T(8,128)} %param.20) | data formatting | bytes 2048 | tf_op args[8]
  2.0 1.4 %copy.16.scores = f32[32,8]{1,0:T(8,128)} copy(f32[32,8]{0,1:T(8,128)} %param.21) | data formatting | bytes 2048 | tf_op args[9]
  3.4 13.1 %shard_map.139 = (bf16[128,384]{1,0:T(8,128)(2,1)}, f32[8,32,128]{2,1,0:T(8,128)}) custom-call(bf16[128,1536]{1,0:T(8,128)(2,1)} %hidden.3, bf16[32,128]{1,0:T(8,128)(2,1)} %key_own.1, bf16[32,128]{1,0:T(8,128)(2,1)} %value_own.1, s32[1,128]{1,0:T(1,128)} %docs.1, s32[32,8]{1,0:T(8,128)} %copy.15.routes, f32[32,8]{1,0:T(8,128)} %copy.16.scores, ...), custom_call_target="tpu_custom_call" | custom-call | tf_op jit(solution)/shard_map/pallas_call | solution.py:217
  16.4 43.7 %shard_map.140 = (bf16[32,1536]{1,0:T(8,128)(2,1)}, bf16[32,1536]{1,0:T(8,128)(2,1)}, bf16[32,1536]{1,0:T(8,128)(2,1)}) custom-call(bf16[128,384]{1,0:T(8,128)(2,1)} %get-tuple-element.5.attended, bf16[128,1536]{1,0:T(8,128)(2,1)} %hidden.3, f32[8,32,128]{2,1,0:T(8,128)} %get-tuple-element.6.gate_all, bf16[384,1536]{1,0:T(8,128)(2,1)} %w_out_hbm.1, ...), custom_call_target="tpu_custom_call" | custom-call | tf_op jit(solution)/shard_map/pallas_call | solution.py:423
  60.1 1.5 %copy.20 = bf16[32,1536]{1,0:T(8,128)(2,1)} copy(bf16[32,1536]{1,0:T(8,128)(2,1)} %get-tuple-element.10) | data formatting | bytes 196608
  61.6 1.5 %copy.21 = bf16[32,1536]{1,0:T(8,128)(2,1)} copy(bf16[32,1536]{1,0:T(8,128)(2,1)} %get-tuple-element.11) | data formatting | bytes 196608
  63.2 1.5 %copy.22 = bf16[32,1536]{1,0:T(8,128)(2,1)} copy(bf16[32,1536]{1,0:T(8,128)(2,1)} %get-tuple-element.12) | data formatting | bytes 196608

commit v5 on v4

--- a/solution.py
+++ b/solution.py
@@ -50,13 +50,13 @@
 
 def attend_kernel(
     n,
-    hidden, key_own, value_own, docs, routes, scores, wq_hbm, wk_hbm, wv_hbm,
+    hidden, key_own, value_own, docs, gates, wq_hbm, wk_hbm, wv_hbm,
     attended, gate_all,
     wq, wk, wv, packed, key_all, value_all, gates_in, w_sem, send, recv,
 ):
     half, ahead, _ = peers(n)
     block = hidden.shape[0]
-    rows = routes.shape[0]
+    rows = gate_all.shape[1]
     share = key_own.shape[0]
     head_size = HEAD_WIDTH
     kv_local = wk.shape[1] // head_size
@@ -75,10 +75,7 @@
     each(1, half, lambda step: greet(0, step))
     each(0, half, lambda step: greet(1, step))
 
-    lanes_g = lax.broadcasted_iota(jnp.int32, (rows, 128), 1)
-    dense = jnp.zeros((rows, 128), F32)
-    for k in range(routes.shape[1]):
-        dense = dense + jnp.where(lanes_g == routes[:, k : k + 1], scores[:, k : k + 1], 0.0)
+    dense = gates[...].T[0:rows]
     tile = dense[0:8]
     for i in range(1, rows // 8):
         tile = tile + pltpu.roll(dense[8 * i : 8 * i + 8], 32 * i, 1)
@@ -210,17 +207,16 @@
     each(0, n, unpack)
 
 
-def attend(n, hidden, key_own, value_own, docs, routes, scores, w_query, key_weight, value_weight):
+def attend(n, hidden, key_own, value_own, docs, gates, rows, w_query, key_weight, value_weight):
     vmem = pl.BlockSpec(memory_space=pltpu.VMEM)
     hbm = pl.BlockSpec(memory_space=pltpu.HBM)
-    rows = routes.shape[0]
     return pl.pallas_call(
         functools.partial(attend_kernel, n),
         out_shape=(
             jax.ShapeDtypeStruct((hidden.shape[0], w_query.shape[1]), BF16),
             jax.ShapeDtypeStruct((n, rows, 128), F32),
         ),
-        in_specs=[vmem] * 6 + [hbm] * 3,
+        in_specs=[vmem] * 5 + [hbm] * 3,
         out_specs=(vmem, vmem),
         scratch_shapes=[
             pltpu.VMEM(w_query.shape, BF16),
@@ -237,7 +233,7 @@
         compiler_params=pltpu.CompilerParams(
             collective_id=0, has_side_effects=True, vmem_limit_bytes=60 << 20
         ),
-    )(hidden, key_own, value_own, docs, routes, scores, w_query, key_weight, value_weight)
+    )(hidden, key_own, value_own, docs, gates, w_query, key_weight, value_weight)
 
 
 def tail_kernel(
@@ -473,8 +469,12 @@
     expert_out,
 ):
     n, n_tp = lax.axis_size("seq"), lax.axis_size("tp")
+    experts = jnp.arange(128, dtype=jnp.int32)
+    picked = routes.T[:, None, :] == experts[None, :, None]
+    gates = jnp.sum(jnp.where(picked, gate_scores.T[:, None, :], 0.0), axis=0)
+    gates = jnp.pad(gates, ((0, 0), (0, 128 - routes.shape[0])))
     attended, gate_all = attend(
-        n, hidden_in, cached_prefix_keys, cached_prefix_values, doc_ids, routes, gate_scores,
+        n, hidden_in, cached_prefix_keys, cached_prefix_values, doc_ids, gates, routes.shape[0],
         w_query, key_weight, value_weight,
     )
     return tail(n, n_tp, attended, w_out, hidden_in, gate_all, expert_in, expert_out)

time: 65 us -> 63.8 us (0.982)
  local copies, waits for them, and re-layouts: 7.35 us -> 5.36 us
  other arithmetic: 0 us -> 0.84 us
    unnamed x5 -> x3, local copies, waits for them, and re-layouts: 7.35 us -> 4.62 us
    reduce_sum x0 -> x1, other arithmetic: none -> 0.84 us  [body(): gates = jnp.sum(jnp.where(picked, gate_scores.T[:, None, :], 0.0), axis=0)]
where the time goes in v5:
time: 63.8 us; the launch traced here: 63.6 us
  Pallas kernels  56.7 us (89%)
  local copies, waits for them, and re-layouts  5.36 us (8%)
  other arithmetic  0.84 us (1%)
  between operations  0.65 us (1%)
    pallas_call x1, Pallas kernels, tail(): pl.pallas_call(functools.partial(tail_kernel, n, n_tp, hparts), out_shape...  43.7 us
    pallas_call x1, Pallas kernels, attend(): pl.pallas_call(functools.partial(attend_kernel, n), out_shape=(jax.ShapeD...  13 us
    unnamed x3, local copies, waits for them, and re-layouts  4.62 us

profile of v5, /device:TPU:0, one launch (start us, length us, event | category | flops | bytes accessed | tf_op | source)
XLA Modules:
  0.0 63.6 jit_solution(4636455386800174221)
XLA Ops:
  0.6 0.8 %select_reduce_fusion = f32[128,32]{0,1:T(8,128)S(1)} fusion(f32[8,32]{1,0:T(8,128)} %bitcast.2, s32[8,32]{1,0:T(8,128)} %bitcast.3), kind=kLoop, calls=%fused_computation | loop fusion | flops 94208 | bytes 18432 | tf_op jit(solution)/shard_map/reduce_sum | solution.py:474
  1.5 0.1 copy.15
  1.6 0.6 %pad.4.gates = f32[128,128]{1,0:T(8,128)} pad(f32[128,32]{1,0:T(8,128)S(1)} %copy.15, f32[]{:T(128)} %constant.1.clone.1), padding=0_0x0_96 | pad | bytes 81924 | tf_op jit(solution)/shard_map/jit(_pad)/pad | solution.py:475
  2.2 13.0 %shard_map.139 = (bf16[128,384]{1,0:T(8,128)(2,1)}, f32[8,32,128]{2,1,0:T(8,128)}) custom-call(bf16[128,1536]{1,0:T(8,128)(2,1)} %hidden.3, bf16[32,128]{1,0:T(8,128)(2,1)} %key_own.1, bf16[32,128]{1,0:T(8,128)(2,1)} %value_own.1, s32[1,128]{1,0:T(1,128)} %docs.1, f32[128,128]{1,0:T(8,128)} %pad.4.gates, bf16[1536,384]{1,0:T(8,128)(2,1)} %wq_hbm.1, ...), custom_call_target="tpu_custom_call" | custom-call | tf_op jit(solution)/shard_map/pallas_call | solution.py:213
  15.3 43.7 %shard_map.140 = (bf16[32,1536]{1,0:T(8,128)(2,1)}, bf16[32,1536]{1,0:T(8,128)(2,1)}, bf16[32,1536]{1,0:T(8,128)(2,1)}) custom-call(bf16[128,384]{1,0:T(8,128)(2,1)} %get-tuple-element.5.attended, bf16[128,1536]{1,0:T(8,128)(2,1)} %hidden.3, f32[8,32,128]{2,1,0:T(8,128)} %get-tuple-element.6.gate_all, bf16[384,1536]{1,0:T(8,128)(2,1)} %w_out_hbm.1, ...), custom_call_target="tpu_custom_call" | custom-call | tf_op jit(solution)/shard_map/pallas_call | solution.py:419
  58.9 1.5 %copy.19 = bf16[32,1536]{1,0:T(8,128)(2,1)} copy(bf16[32,1536]{1,0:T(8,128)(2,1)} %get-tuple-element.10) | data formatting | bytes 196608
  60.5 1.5 %copy.20 = bf16[32,1536]{1,0:T(8,128)(2,1)} copy(bf16[32,1536]{1,0:T(8,128)(2,1)} %get-tuple-element.11) | data formatting | bytes 196608
  62.0 1.5 %copy.21 = bf16[32,1536]{1,0:T(8,128)(2,1)} copy(bf16[32,1536]{1,0:T(8,128)(2,1)} %get-tuple-element.12) | data formatting | bytes 196608
